TPU v7x, 32 devices: a whole 2x2x4 slice. The times are simulated.
32 devices in a mesh: grp: 4 (over y, core), nbr: 8 (over z, x).
Axes of the slice: x: 2, y: 2, z: 4, core: 2. Of those that a mesh axis runs over, the one named last changes fastest.
Arguments:
- sims: float32 [512, 128, 128], P(('grp', 'nbr')), may hold values from -6 to 6
- own_tiles: float32 [6144, 128, 128], P(('grp', 'nbr')), may hold values from -0.15625 to 0.15625
- own_cols: int32 [6144], P(('grp', 'nbr')), may hold values from 0 to 143
- own_rows: int32 [6144], P(('grp', 'nbr')), may hold values from 0 to 15
- help_tiles: float32 [512, 128, 128], P(('grp', 'nbr')), may hold values from -0.15625 to 0.15625
- help_cols: int32 [512], P(('grp', 'nbr')), may hold values from 0 to 143
- help_rows: int32 [512], P(('grp', 'nbr')), may hold values from 0 to 15
- help_live: int32 [512], P(('grp', 'nbr')), may hold values from 0 to 1, as said below
Outputs:
- reobserved: float32 [512, 128, 128], P(('grp', 'nbr'))
Inputs may be any that keep to these rules, and one draw needn't show every extreme that they name: `help_live`: helper slot j of a device serves the owner of neighbour index j // 2 in the same group, so at most 2 live slots go from one device to one owner; in every group one owner receives all 2 slots live from every device of the group.
All inputs are finite; a program needn't handle non-finite values.
Results may differ from a plain program's by a relative error of at most 0.0001.
Values sent between devices are 32-bit elements; how exact they have to be, the bound alone decides.
No kernel may reach another device: no remote copies, remote signals or barrier semaphores. Data moves between devices by JAX's collectives and lax.ppermute only.
A program may use at most 192 MiB of HBM per device.

v0:
```python
import jax
import jax.numpy as jnp
from jax import lax
from jax.sharding import PartitionSpec as P

RIM = 8


def padded(shard, sides, width):
    for axis, dim in sides:
        peers, length = (lax.axis_size(axis), shard.shape[dim])
        up = [(i, (i + 1) % peers) for i in range(peers - 1)]
        down = [(j, i) for i, j in up]
        last = lax.slice_in_dim(shard, length - width, length, axis=dim)
        initial = lax.slice_in_dim(shard, 0, width, axis=dim)
        before = lax.ppermute(last, axis, up)
        after = lax.ppermute(initial, axis, down)
        shard = jnp.concatenate([before, shard, after], axis=dim)
    return shard


def pick_from(source, first, cols):
    length = source.shape[0]
    index = cols - first
    valid = ((index >= 0) & (index < length)).astype(jnp.float32)
    taken = jnp.take(source, jnp.clip(index, 0, length - 1), axis=0)
    return taken * valid[:, None, None]


def local(sims, own_tiles, own_cols, own_rows, help_tiles, help_cols, help_rows, help_live):
    high = lax.Precision.HIGHEST
    rows_dev = sims.shape[0]
    neighbours = lax.axis_size("nbr")
    group_rows = rows_dev * neighbours
    help_dev = help_tiles.shape[0]
    slots_owner = help_dev // neighbours
    group = lax.all_gather(sims, "nbr", axis=0, tiled=True)
    own_pick = pick_from(group, RIM, own_cols)
    help_pick = pick_from(group, RIM, help_cols)
    edges = jnp.concatenate([group[:RIM], group[group_rows - RIM :]], axis=0)
    rims = padded(edges, (("grp", 0),), RIM)
    lower = rims[:RIM]
    upper = rims[rims.shape[0] - RIM :]
    own_pick = (
        own_pick + pick_from(lower, 0, own_cols) + pick_from(upper, RIM + group_rows, own_cols)
    )
    help_pick = (
        help_pick + pick_from(lower, 0, help_cols) + pick_from(upper, RIM + group_rows, help_cols)
    )
    own_terms = jnp.einsum("tij,tjs->tis", own_tiles, own_pick, precision=high)
    select = (own_rows[None, :] == jnp.arange(rows_dev, dtype=jnp.int32)[:, None]).astype(
        jnp.float32
    )
    own_sum = jnp.einsum("rt,tis->ris", select, own_terms, precision=high)
    help_terms = (
        jnp.einsum("tij,tjs->tis", help_tiles, help_pick, precision=high)
        * help_live.astype(jnp.float32)[:, None, None]
    )
    outgoing = help_terms.reshape(neighbours, slots_owner, help_terms.shape[1], help_terms.shape[2])
    out_rows = help_rows.astype(jnp.float32).reshape(neighbours, slots_owner)
    incoming, in_rows = (
        lax.all_to_all(outgoing, "nbr", split_axis=0, concat_axis=0, tiled=True),
        lax.all_to_all(out_rows, "nbr", split_axis=0, concat_axis=0, tiled=True),
    )
    flat_terms = incoming.reshape(help_dev, incoming.shape[2], incoming.shape[3])
    flat_rows = in_rows.reshape(help_dev)
    picker = (flat_rows[None, :] == jnp.arange(rows_dev, dtype=jnp.float32)[:, None]).astype(
        jnp.float32
    )
    help_sum = jnp.einsum("rt,tis->ris", picker, flat_terms, precision=high)
    return own_sum + help_sum


def solution(mesh):
    placed = (
        P(("grp", "nbr"), None, None),
        P(("grp", "nbr"), None, None),
        P(("grp", "nbr")),
        P(("grp", "nbr")),
        P(("grp", "nbr"), None, None),
        P(("grp", "nbr")),
        P(("grp", "nbr")),
        P(("grp", "nbr")),
    )
    return jax.shard_map(
        local, mesh=mesh, in_specs=placed, out_specs=P(("grp", "nbr"), None, None), check_vma=False
    )
```

profile of v0, /device:TPU:27, one launch (start us, length us, event | category | flops | bytes accessed | tf_op | source)
XLA Modules:
  0.0 252.7 jit_solution(12827483655304515915)
XLA Ops:
  6.5 0.7 all-gather.2.cloned.1.call-update
  7.9 0.7 all_to_all.9
  8.6 5.4 %all-to-all-start = ((f32[8,1,2]{2,1,0:T(1,128)}), f32[8,1,2]{2,1,0:T(1,128)S(1)}, u32[]{:S(2)}, u32[]{:S(2)}) async-start(f32[8,1,2]{2,1,0:T(1,128)} %bitcast.2), calls=%async_computation | async-start | bytes 8192 | tf_op jit(solution)/shard_map/all_to_all | solution.py:63
  14.0 0.7 compare_select_fusion.1
  14.7 0.7 and_convert_fusion.2
  15.4 117.3 %all-gather.2.cloned.1.call-done = f32[128,128,128]{2,1,0:T(8,128)} async-done(((f32[16,128,128]{2,1,0:T(8,128)}), f32[128,128,128]{2,1,0:T(8,128)}) %all-gather.2.cloned.1.call-update) | async-done | bytes 8388624 | tf_op jit(solution)/shard_map/all_gather | solution.py:37
  132.7 2.3 fusion.39
  135.0 3.5 %collective-permute-start = (f32[8,128,128]{2,1,0:T(8,128)}, f32[8,128,128]{2,1,0:T(8,128)S(1)}, u32[]{:S(2)}, u32[]{:S(2)}) collective-permute-start(f32[8,128,128]{2,1,0:T(8,128)} %get-tuple-element.17), channel_id=1, source_target_pairs={{0,8},{8,16},{16,24},{1,9},{9,17},{17,25},{2,10},{10,18},{18,26},{... | collective-permute-start | bytes 1572872 | tf_op jit(solution)/shard_map/ppermute | solution.py:16
  138.5 1.9 collective-permute-start.1
  140.4 0.7 compare_and_fusion.3
  143.1 4.0 %gather_fusion.1 = f32[16,128,128]{2,1,0:T(8,128)S(1)} fusion(f32[128,128,128]{2,1,0:T(8,128)} %all-gather.2.cloned.1.call-done, s32[1024]{0:T(1024)S(1)} %pad_clamp_fusion.2), kind=kCustom, calls=%fused_computation.5 | custom fusion | bytes 2097216 | tf_op jit(solution)/shard_map/jit(_take)/gather | solution.py:26
  147.1 14.1 %gather_fusion = f32[192,128,128]{2,1,0:T(8,128)} fusion(f32[128,128,128]{2,1,0:T(8,128)} %all-gather.2.cloned.1.call-done, s32[1024]{0:T(1024)S(1)} %get-tuple-element.37), kind=kCustom, calls=%fused_computation.4 | custom fusion | bytes 25166592 | tf_op jit(solution)/shard_map/jit(_take)/gather | solution.py:26
  161.2 1.6 gather_fusion.5
  162.7 1.7 gather_fusion.4
  164.4 4.7 %convolution_multiply_fusion = f32[16,128,128]{2,1,0:T(8,128)} fusion(f32[16,128,128]{2,1,0:T(8,128)S(1)} %copy-done, f32[16,128,128]{2,1,0:T(8,128)} %gather_fusion.5, f32[16,128,128]{2,1,0:T(8,128)} %gather_fusion.4, f32[16,128,128]{2,1,0:T(8,128)S(1)} %gather_fusion.1, f32[16]{0:T(128)S(1)} %convert_element_type.33, f32[16]{0:T(128)S(1)} %get-tuple-element.28, ...), kind=kOutput, calls=%fused_computation.22 | convolution fusion | flops 405012480 | bytes 5243184 | tf_op jit(solution)/shard_map/tij,tjs->tis/dot_general | solution.py:56
  169.1 6.6 %all-to-all-start.1 = ((f32[8,2,128,128]{2,3,1,0:T(8,128)}), f32[8,2,128,128]{2,3,1,0:T(8,128)S(1)}, u32[]{:S(2)}, u32[]{:S(2)}) async-start(f32[8,2,128,128]{2,3,1,0:T(8,128)} %bitcast.18), calls=%async_computation.1 | async-start | bytes 2097152 | tf_op jit(solution)/shard_map/all_to_all | solution.py:62
  175.6 5.8 %gather_fusion.2 = f32[192,128,128]{2,1,0:T(8,128)} fusion(f32[8,128,128]{2,1,0:T(8,128)S(1)} %collective-permute-done, s32[1024]{0:T(1024)S(1)} %pad_clamp_fusion.4), kind=kCustom, calls=%fused_computation.clone | custom fusion | bytes 25166592 | tf_op jit(solution)/shard_map/jit(_take)/gather | solution.py:26
  181.5 6.0 %gather_fusion.3 = f32[192,128,128]{2,1,0:T(8,128)} fusion(f32[8,128,128]{2,1,0:T(8,128)S(1)} %collective-permute-done.1, s32[1024]{0:T(1024)S(1)} %get-tuple-element.36), kind=kCustom, calls=%fused_computation.2.clone | custom fusion | bytes 25166592 | tf_op jit(solution)/shard_map/jit(_take)/gather | solution.py:26
  187.4 33.8 %fusion.14 = f32[192,128,128]{1,2,0:T(8,128)} fusion(f32[192,128,128]{2,1,0:T(8,128)} %param.13, f32[192,128,128]{2,1,0:T(8,128)} %gather_fusion.3, f32[192,128,128]{2,1,0:T(8,128)} %gather_fusion.2, f32[192,128,128]{2,1,0:T(8,128)} %gather_fusion, f32[192]{0:T(256)S(1)} %get-tuple-element.21, f32[192]{0:T(256)S(1)} %get-tuple-element.26, ...), kind=kOutput, calls=%fused_computation.20 | convolution fusion | flops 4857004032 | bytes 62917440 | tf_op jit(solution)/shard_map/tij,tjs->tis/dot_general | solution.py:50
  221.2 12.8 %copy.16 = f32[192,128,128]{2,0,1:T(8,128)} copy(f32[192,128,128]{1,2,0:T(8,128)} %fusion.14) | data formatting | bytes 25165824 | tf_op jit(solution)/shard_map/tij,tjs->tis/dot_general | solution.py:50
  234.1 7.9 %fusion.31 = f32[16,128,128]{2,0,1:T(8,128)} fusion(f32[192,128,128]{2,0,1:T(8,128)} %copy.16, s32[192]{0:T(256)S(1)} %copy-done.2), kind=kOutput, calls=%fused_computation.38 | convolution fusion | flops 603982848 | bytes 13632256 | tf_op jit(solution)/shard_map/rt,tis->ris/dot_general | solution.py:54
  241.9 0.8 copy.19
  242.7 1.8 convolution_add_fusion
  244.6 1.3 copy.20
  (20 shorter events, 2.6 us)
Async XLA Ops:
  6.5 157.9 %copy-start = (f32[16,128,128]{2,1,0:T(8,128)S(1)}, f32[16,128,128]{2,1,0:T(8,128)}, u32[]{:S(2)}) copy-start(f32[16,128,128]{2,1,0:T(8,128)} %param.16) | copy-start | bytes 3145732
  6.5 126.2 %all-gather.2.cloned.1.call-start = ((), (), s32[]{:S(2)}) async-start(), calls=%async_computation.2 | async-start | bytes 9437184 | tf_op jit(solution)/shard_map/all_gather | solution.py:37
  8.6 133.2 %all-to-all-start = ((f32[8,1,2]{2,1,0:T(1,128)}), f32[8,1,2]{2,1,0:T(1,128)S(1)}, u32[]{:S(2)}, u32[]{:S(2)}) async-start(f32[8,1,2]{2,1,0:T(1,128)} %bitcast.2), calls=%async_computation | async-start | bytes 8192 | tf_op jit(solution)/shard_map/all_to_all | solution.py:63
  135.0 27.8 %collective-permute-start = (f32[8,128,128]{2,1,0:T(8,128)}, f32[8,128,128]{2,1,0:T(8,128)S(1)}, u32[]{:S(2)}, u32[]{:S(2)}) collective-permute-start(f32[8,128,128]{2,1,0:T(8,128)} %get-tuple-element.17), channel_id=1, source_target_pairs={{0,8},{8,16},{16,24},{1,9},{9,17},{17,25},{2,10},{10,18},{18,26},{... | collective-permute-start | bytes 1572872 | tf_op jit(solution)/shard_map/ppermute | solution.py:16
  138.5 22.7 %collective-permute-start.1 = (f32[8,128,128]{2,1,0:T(8,128)}, f32[8,128,128]{2,1,0:T(8,128)S(1)}, u32[]{:S(2)}, u32[]{:S(2)}) collective-permute-start(f32[8,128,128]{2,1,0:T(8,128)} %get-tuple-element.18), channel_id=1, source_target_pairs={{8,0},{16,8},{24,16},{9,1},{17,9},{25,17},{10,2},{18,10},{26,18},{... | collective-permute-start | bytes 1572872 | tf_op jit(solution)/shard_map/ppermute | solution.py:17
  169.1 72.9 %all-to-all-start.1 = ((f32[8,2,128,128]{2,3,1,0:T(8,128)}), f32[8,2,128,128]{2,3,1,0:T(8,128)S(1)}, u32[]{:S(2)}, u32[]{:S(2)}) async-start(f32[8,2,128,128]{2,3,1,0:T(8,128)} %bitcast.18), calls=%async_computation.1 | async-start | bytes 2097152 | tf_op jit(solution)/shard_map/all_to_all | solution.py:62
  221.2 12.8 %copy-start.2 = (s32[192]{0:T(256)S(1)}, s32[192]{0:T(256)}, u32[]{:S(2)}) copy-start(s32[192]{0:T(256)} %param.15) | copy-start | bytes 2308
  221.2 24.7 %copy-start.1 = (f32[16,128,128]{2,1,0:T(8,128)S(1)}, f32[16,128,128]{2,1,0:T(8,128)}, u32[]{:S(2)}) copy-start(f32[16,128,128]{2,1,0:T(8,128)} %param.16) | copy-start | bytes 3145732
Sparse Core Ops, SparseCore 0:
  9.5 123.1 all-gather.1
where the time goes:
time: 255 us; the launch traced here: 253 us
  waiting for transfers between devices  118 us (46%)
  local copies, waits for them, and re-layouts  51.6 us (20%)
  matrix products  48.2 us (19%)
  starting transfers between devices  17.4 us (7%)
  between operations  13.5 us (5%)
  other arithmetic  4.04 us (2%)
    all_gather x1, waiting for transfers between devices, local(): group = lax.all_gather(sims, 'nbr', axis=0, tiled=True)  117 us
    dot_general x1, matrix products, local(): own_terms = jnp.einsum('tij,tjs->tis', own_tiles, own_pick, precision=high)  33.8 us
    gather x6, local copies, waits for them, and re-layouts, pick_from(): taken = jnp.take(source, jnp.clip(index, 0, length - 1), axis=0)  33.1 us
    dot_general x1, local copies, waits for them, and re-layouts, local(): own_terms = jnp.einsum('tij,tjs->tis', own_tiles, own_pick, precision=high)  12.8 us
    dot_general x1, matrix products, local(): own_sum = jnp.einsum('rt,tis->ris', select, own_terms, precision=high)  7.86 us
    all_to_all x1, starting transfers between devices, local(): lax.all_to_all(outgoing, 'nbr', split_axis=0, concat_axis=0, tiled=True)  6.56 us
    all_to_all x1, starting transfers between devices, local(): lax.all_to_all(out_rows, 'nbr', split_axis=0, concat_axis=0, tiled=True)  5.44 us
  transfers between devices with their start and end apart: 5, of which 1 were waited for; matrix products, arithmetic and copies ran while one was open for 37% of the time, Pallas kernels for 0%

commit v1 on v0

v1 whole, which is shorter than its diff:
```python
import functools

import jax
import jax.numpy as jnp
import numpy as np
from jax import lax
from jax.experimental import pallas as pl
from jax.experimental.pallas import tpu as pltpu
from jax.sharding import PartitionSpec as P

RIM = 8
UNROLL = 4
DEPTH = 4
VMEM_BYTES = 40 << 20
HIGH = lax.Precision.HIGHEST
F32 = jnp.float32
I32 = jnp.int32


def grid_of(mesh):
    count = mesh.shape["nbr"]
    try:
        where = np.array([d.coords for d in mesh.devices[0]])
    except AttributeError:
        return [(i, 0) for i in range(count)]
    axes = [a for a in range(where.shape[1]) if len(set(where[:, a])) > 1]
    if len(axes) != 2:
        return [(i, 0) for i in range(count)]
    first, second = axes
    if len(set(where[:, second])) > len(set(where[:, first])):
        first, second = second, first
    where = where - where.min(axis=0)
    return [(int(w[first]), int(w[second])) for w in where]


def ring_of(places):
    index = {place: n for n, place in enumerate(places)}
    rows = max(p[0] for p in places) + 1
    cols = max(p[1] for p in places) + 1
    if len(index) != rows * cols or rows % 2 or cols < 2:
        return list(range(len(places)))
    walk = [(r, 0) for r in range(rows)]
    for step, r in enumerate(reversed(range(rows))):
        across = range(1, cols) if step % 2 == 0 else reversed(range(1, cols))
        walk += [(r, c) for c in across]
    return [index[w] for w in walk]


class Plan:
    def __init__(self, mesh):
        self.groups = mesh.shape["grp"]
        self.count = mesh.shape["nbr"]
        places = grid_of(mesh)
        self.ring = ring_of(places)
        self.pos = [self.ring.index(n) for n in range(self.count)]
        self.half = self.count // 2
        count, half = self.count, self.half
        self.right = self.around([(i, (i + 1) % count) for i in range(count)])
        self.left = self.around([(i, (i - 1) % count) for i in range(count)])
        near = lambda a, b: sum(abs(u - v) for u, v in zip(places[self.ring[a]], places[self.ring[b]])) == 1
        self.cross_r, self.cross_l = {}, {}
        for i in range(count):
            over_r, over_l = (i + half + 1) % count, (i + half - 1) % count
            if half > 2 and near(i, over_r) and over_r not in self.cross_r.values():
                self.cross_r[i] = over_r
            elif half > 2 and near(i, over_l) and over_l not in self.cross_l.values():
                self.cross_l[i] = over_l
        self.ends = [i for i in range(count) if i not in self.cross_r and i not in self.cross_l]
        self.pairs_r = self.around([(s, i) for i, s in self.cross_r.items()])
        self.pairs_l = self.around([(s, i) for i, s in self.cross_l.items()])
        self.end_right = self.around([((i - 1) % count, i) for i in self.ends])
        self.end_left = self.around([((i + 1) % count, i) for i in self.ends])

    def around(self, pairs):
        return [(self.ring[a], self.ring[b]) for a, b in pairs]

    def between(self, step, keep):
        return [
            (g * self.count + self.ring[i], (g + step) * self.count + self.ring[i])
            for g in range(self.groups)
            if 0 <= g + step < self.groups
            for i in keep
        ]


def copy_in(pieces, place, sem):
    return [
        pltpu.make_async_copy(ref, place.at[pl.ds(at, ref.shape[0])], sem.at[k])
        for k, (ref, at) in enumerate(pieces)
    ]


def run_tiles(offs, info, stage, bits, tiles, xs, acc, buf, sems, ready):
    slot_bits, row_bits = bits
    total = info.shape[0]
    dump = acc.shape[0] - 1
    first, last = offs[stage], offs[stage + 1]
    groups = lax.div(last - first + (UNROLL - 1), UNROLL)

    def fetch(g):
        s = lax.rem(g, DEPTH)
        for u in range(UNROLL):
            at = jnp.minimum(first + g * UNROLL + u, total - 1)
            tile = lax.shift_right_logical(info[at], slot_bits + row_bits)
            pltpu.make_async_copy(tiles.at[tile], buf.at[s, u], sems.at[s]).start()

    for g in range(DEPTH - 1):
        pl.when(g < groups)(functools.partial(fetch, jnp.int32(g)))
    ready()

    def body(g, carry):
        s = lax.rem(g, DEPTH)
        pl.when(g + DEPTH - 1 < groups)(lambda: fetch(g + DEPTH - 1))
        for u in range(UNROLL):
            pltpu.make_async_copy(tiles.at[0], buf.at[s, u], sems.at[s]).wait()
        rows, terms = [], []
        for u in range(UNROLL):
            at = first + g * UNROLL + u
            entry = info[jnp.minimum(at, total - 1)]
            row = lax.shift_right_logical(entry, slot_bits) & ((1 << row_bits) - 1)
            slot = entry & ((1 << slot_bits) - 1)
            rows.append(jnp.where(at < last, row, dump))
            terms.append(jnp.dot(buf[s, u], xs[slot], precision=HIGH, preferred_element_type=F32))
        for row, term in zip(rows, terms):
            acc[row] += term
        return carry

    lax.fori_loop(0, groups, body, 0)


def stage_kernel(stage, bits, have, offs, info, *refs):
    refs = list(refs)
    shards = [refs.pop(0) for _ in range(have)]
    tiles = refs.pop(0)
    before = refs.pop(0) if stage else None
    acc, xs, buf, xsems, sems = refs
    starts = np.cumsum([0] + [s.shape[0] for s in shards])
    copies = copy_in(list(zip(shards, starts)), xs, xsems)
    for c in copies:
        c.start()

    def ready():
        acc[...] = jnp.zeros_like(acc) if before is None else before[...]
        for c in copies:
            c.wait()

    run_tiles(offs, info, stage, bits, tiles, xs, acc, buf, sems, ready)


def last_stage_kernel(stage, bits, rows, modes, offs, info, mode, hbuf, hidx, *refs):
    refs = list(refs)
    sources = [refs.pop(0) for _ in range(len(refs) - 8)]
    tiles, before, acc, hx, xs, buf, xsems, sems = refs
    far_a, far_b, far_r, far_l, low_near, low_far, up_near, up_far = sources[-8:]
    half = far_a.shape[0]
    slots = hx.shape[0]

    def gather(j, carry):
        for k, source in enumerate(sources):
            @pl.when(hbuf[j] == k)
            def _():
                pltpu.make_async_copy(source.at[hidx[j]], hx.at[j], xsems.at[4]).start()
        return carry

    lax.fori_loop(0, slots, gather, 0)

    def bring(ref, at, k):
        pltpu.make_async_copy(ref, xs.at[pl.ds(at, ref.shape[0])], xsems.at[k]).start()

    @pl.when(mode[0] == 0)
    def _():
        bring(far_a, 0, 0)
        bring(far_b, half, 1)

    @pl.when(mode[0] == 1)
    def _():
        bring(far_r.at[pl.ds(0, half)], 0, 0)
        bring(far_r.at[pl.ds(half, half)], half, 1)

    @pl.when(mode[0] == 2)
    def _():
        bring(far_l.at[pl.ds(0, half)], 0, 0)
        bring(far_l.at[pl.ds(half, half)], half, 1)

    @pl.when(mode[1] == 0)
    def _():
        bring(low_near, rows, 2)

    @pl.when(mode[1] == 1)
    def _():
        bring(low_far, rows, 2)

    @pl.when(mode[2] == 0)
    def _():
        bring(up_near, rows + RIM, 3)

    @pl.when(mode[2] == 1)
    def _():
        bring(up_far, rows + RIM, 3)

    def ready():
        acc[...] = before[...]
        pltpu.make_async_copy(far_a, xs.at[pl.ds(0, half)], xsems.at[0]).wait()
        pltpu.make_async_copy(far_b, xs.at[pl.ds(half, half)], xsems.at[1]).wait()
        pltpu.make_async_copy(low_near, xs.at[pl.ds(rows, RIM)], xsems.at[2]).wait()
        pltpu.make_async_copy(up_near, xs.at[pl.ds(rows + RIM, RIM)], xsems.at[3]).wait()

    run_tiles(offs, info, stage, bits, tiles, xs, acc, buf, sems, ready)

    def drain(j, carry):
        pltpu.make_async_copy(sources[0].at[0], hx.at[j], xsems.at[4]).wait()
        return carry

    lax.fori_loop(0, slots, drain, 0)


def help_kernel(hrow, tiles, xs, before, out, acc):
    rows = out.shape[0]
    acc[...] = before[...]

    def body(g, carry):
        terms = []
        for u in range(2):
            j = g * 2 + u
            terms.append(jnp.dot(tiles[j], xs[j], precision=HIGH, preferred_element_type=F32))
        for u in range(2):
            acc[hrow[g * 2 + u]] += terms[u]
        return carry

    lax.fori_loop(0, tiles.shape[0] // 2, body, 0)
    if tiles.shape[0] % 2:
        j = tiles.shape[0] - 1
        acc[hrow[j]] += jnp.dot(tiles[j], xs[j], precision=HIGH, preferred_element_type=F32)
    out[...] = acc[pl.ds(0, rows)]


def edge_kernel(count, mode, *refs):
    refs = list(refs)
    low, up, sems = refs[-3:]
    shards = refs[:-3]
    size = shards[0].shape[0]

    def pick(k, ref):
        @pl.when(mode[3] == k)
        def _():
            pltpu.make_async_copy(ref.at[pl.ds(size - RIM, RIM)], low, sems.at[0]).start()

        @pl.when(mode[4] == k)
        def _():
            pltpu.make_async_copy(ref.at[pl.ds(0, RIM)], up, sems.at[1]).start()

    for k, ref in enumerate(shards):
        pick(k, ref)
    pltpu.make_async_copy(shards[0].at[pl.ds(0, RIM)], low, sems.at[0]).wait()
    pltpu.make_async_copy(shards[0].at[pl.ds(0, RIM)], up, sems.at[1]).wait()


def bits_for(n):
    return max(1, (n - 1).bit_length())


SMEM = pl.BlockSpec(memory_space=pltpu.SMEM)
ANY = pl.BlockSpec(memory_space=pl.ANY)
VMEM = pl.BlockSpec(memory_space=pltpu.VMEM)


def local(plan, sims, own_tiles, own_cols, own_rows, help_tiles, help_cols, help_rows, help_live):
    rows, side, width = sims.shape
    count, half = plan.count, plan.half
    group_rows = rows * count
    cut = rows // 2
    total = own_tiles.shape[0]
    slots = help_tiles.shape[0]
    per_stage = max(2 * rows, rows + 2 * RIM)
    bits = (bits_for(per_stage), bits_for(rows))
    both = ("grp", "nbr")

    me = lax.axis_index("nbr")
    table = lambda values, index: sum(
        jnp.where(index == k, I32(v), I32(0)) for k, v in enumerate(values)
    )
    here = table(plan.pos, me)

    from_left, from_right = [sims], [sims]
    for _ in range(1, half):
        from_left.append(lax.ppermute(from_left[-1], "nbr", plan.right))
        from_right.append(lax.ppermute(from_right[-1], "nbr", plan.left))
    far_r = lax.ppermute(from_left[1], "nbr", plan.pairs_r)
    far_l = lax.ppermute(from_right[1], "nbr", plan.pairs_l)
    far_a = lax.ppermute(from_left[-1][:cut], "nbr", plan.end_right)
    far_b = lax.ppermute(from_right[-1][cut:], "nbr", plan.end_left)

    notes = jnp.stack([help_cols, help_rows, help_live], axis=1)
    notes = lax.all_to_all(notes, "nbr", split_axis=0, concat_axis=0, tiled=True)
    in_tiles = lax.all_to_all(help_tiles, "nbr", split_axis=0, concat_axis=0, tiled=True)

    kind_of = lambda members, value: [value if i in members else 0 for i in range(count)]
    far_kind = table([a + b for a, b in zip(kind_of(plan.cross_r, 1), kind_of(plan.cross_l, 2))], here)
    place_low, place_up = plan.pos[count - 1], plan.pos[0]

    def locate(cols):
        block = cols - RIM
        low, up = block < 0, block >= group_rows
        inside = jnp.clip(block, 0, group_rows - 1)
        shard = inside // rows
        index = inside - shard * rows
        ahead = lax.rem(table(plan.pos, shard) - here + count, I32(count))
        stage = jnp.minimum(ahead, count - ahead)
        from_right_side = (ahead > 0) & (ahead < half)
        slot = index + jnp.where(from_right_side, rows, 0)
        rim = low | up
        slot = jnp.where(low, rows + cols, jnp.where(up, rows + RIM + block - group_rows, slot))
        stage = jnp.where(rim, half, stage)
        near_buf = jnp.where(ahead == 0, 0, jnp.where(ahead < half, half - 1 + ahead, count - ahead))
        base = 2 * half - 1
        far_buf = jnp.where(
            far_kind == 0, jnp.where(index < cut, base, base + 1), jnp.where(far_kind == 1, base + 2, base + 3)
        )
        far_idx = jnp.where((far_kind == 0) & (index >= cut), index - cut, index)
        far = ahead == half
        buf = jnp.where(far, far_buf, near_buf)
        idx = jnp.where(far, far_idx, index)
        buf = jnp.where(low, base + 4 + low_far_kind, jnp.where(up, base + 6 + up_far_kind, buf))
        idx = jnp.where(low, cols, jnp.where(up, block - group_rows, idx))
        return stage, slot, buf, idx

    def away(place):
        return lax.rem(I32(place) - here + count, I32(count))

    low_far_kind = (away(place_low) == half).astype(I32)
    up_far_kind = (away(place_up) == half).astype(I32)

    def edge_source(place):
        ahead = away(place)
        near = jnp.where(ahead == 0, 0, jnp.where(ahead < half, half - 1 + ahead, count - ahead))
        return jnp.where(ahead == half, 0, near)

    mode = jnp.stack(
        [far_kind, low_far_kind, up_far_kind, edge_source(place_low), edge_source(place_up)]
    ).astype(I32)

    stage, slot, _, _ = locate(own_cols)
    number = jnp.arange(total, dtype=I32)
    key = (stage * per_stage + slot) * total + number
    rank = jnp.sum((key[None, :] < key[:, None]).astype(I32), axis=1)
    entry = (number << (bits[0] + bits[1])) | (own_rows << bits[0]) | slot
    info = jnp.sum(jnp.where(rank[:, None] == number[None, :], entry[:, None], 0), axis=0)
    offs = jnp.sum(
        (stage[None, :] < jnp.arange(half + 2, dtype=I32)[:, None]).astype(I32), axis=1
    )

    _, _, hbuf, hidx = locate(notes[:, 0])
    hrow = jnp.where(notes[:, 2] > 0, notes[:, 1], rows)

    partial = jax.ShapeDtypeStruct((rows + 1, side, width), F32)
    scratch = lambda more: [
        pltpu.VMEM((per_stage, side, width), F32),
        pltpu.VMEM((DEPTH, UNROLL, side, side), F32),
        pltpu.SemaphoreType.DMA((more,)),
        pltpu.SemaphoreType.DMA((DEPTH,)),
    ]
    params = pltpu.CompilerParams(vmem_limit_bytes=VMEM_BYTES)
    cost = pl.CostEstimate(
        flops=2 * side * side * width * total // count, bytes_accessed=8 << 20, transcendentals=0
    )
    acc = None
    for s in range(half):
        shards = [sims] if s == 0 else [from_left[s], from_right[s]]
        args = [offs, info, *shards, own_tiles] + ([] if s == 0 else [acc])
        acc = pl.pallas_call(
            functools.partial(stage_kernel, s, bits, len(shards)),
            out_shape=partial,
            in_specs=[SMEM, SMEM] + [ANY] * (len(shards) + 1) + ([] if s == 0 else [VMEM]),
            out_specs=VMEM,
            scratch_shapes=scratch(2),
            compiler_params=params,
            cost_estimate=cost,
            name=f"stage{s}",
        )(*args)

    near_shards = [sims] + from_left[1:] + from_right[1:]
    edge = jax.ShapeDtypeStruct((RIM, side, width), F32)
    edge_low, edge_up = pl.pallas_call(
        functools.partial(edge_kernel, count),
        out_shape=(edge, edge),
        in_specs=[SMEM] + [ANY] * len(near_shards),
        out_specs=(ANY, ANY),
        scratch_shapes=[pltpu.SemaphoreType.DMA((2,))],
        name="edges",
    )(mode, *near_shards)
    far_low, far_up = (place_low + half) % count, (place_up + half) % count
    without = lambda i: [k for k in range(count) if k != i]
    low_near = lax.ppermute(edge_low, both, plan.between(1, without(far_low)))
    up_near = lax.ppermute(edge_up, both, plan.between(-1, without(far_up)))

    def far_shard(i, tail):
        if i in plan.cross_r or i in plan.cross_l:
            whole = far_r if i in plan.cross_r else far_l
        elif cut >= RIM:
            whole = far_b if tail else far_a
        else:
            whole = jnp.concatenate([far_a, far_b], axis=0)
        return whole[whole.shape[0] - RIM :] if tail else whole[:RIM]

    low_far = lax.ppermute(far_shard(far_low, True), both, plan.between(1, [far_low]))
    up_far = lax.ppermute(far_shard(far_up, False), both, plan.between(-1, [far_up]))

    sources = near_shards + [far_a, far_b, far_r, far_l, low_near, low_far, up_near, up_far]
    acc, hx = pl.pallas_call(
        functools.partial(last_stage_kernel, half, bits, rows, None),
        out_shape=(partial, jax.ShapeDtypeStruct((slots, side, width), F32)),
        in_specs=[SMEM] * 5 + [ANY] * (len(sources) + 1) + [VMEM],
        out_specs=(VMEM, ANY),
        scratch_shapes=scratch(5),
        compiler_params=params,
        cost_estimate=cost,
        name="last_stage",
    )(offs, info, mode, hbuf, hidx, *sources, own_tiles, acc)

    return pl.pallas_call(
        help_kernel,
        out_shape=jax.ShapeDtypeStruct((rows, side, width), F32),
        in_specs=[SMEM, VMEM, VMEM, VMEM],
        out_specs=VMEM,
        scratch_shapes=[pltpu.VMEM((rows + 1, side, width), F32)],
        compiler_params=params,
        name="help",
    )(hrow, in_tiles, hx, acc)


def solution(mesh):
    spread = P(("grp", "nbr"), None, None)
    flat = P(("grp", "nbr"))
    return jax.shard_map(
        functools.partial(local, Plan(mesh)),
        mesh=mesh,
        in_specs=(spread, spread, flat, flat, spread, flat, flat, flat),
        out_specs=spread,
        check_vma=False,
    )
```

time: 255 us -> 178 us (0.70)
  the two profiles are of different devices: /device:TPU:27 before, /device:TPU:12 now
where the time goes in v1:
time: 178 us; the launch traced here: 177 us
  Pallas kernels  72.7 us (41%)
  waiting for transfers between devices  59.5 us (33%)
  starting transfers between devices  35.3 us (20%)
  local copies, waits for them, and re-layouts  8.91 us (5%)
    ppermute x3, waiting for transfers between devices, local(): from_right.append(lax.ppermute(from_right[-1], 'nbr', plan.left))  45.5 us
    pallas_call x1, Pallas kernels, local(): pl.pallas_call(functools.partial(edge_kernel, count), out_shape=(edge, ed...  33.7 us
    pallas_call x4, Pallas kernels, local(): pl.pallas_call(functools.partial(stage_kernel, s, bits, len(shards)), out...  23.5 us
    all_to_all x1, waiting for transfers between devices, local(): lax.all_to_all(notes, 'nbr', split_axis=0, concat_axis=0, tiled=True)  14 us
    pallas_call x1, Pallas kernels, local(): pl.pallas_call(functools.partial(last_stage_kernel, half, bits, rows, Non...  10.9 us
    all_to_all x1, starting transfers between devices, local(): lax.all_to_all(notes, 'nbr', split_axis=0, concat_axis=0, tiled=True)  6.25 us
    all_to_all x1, starting transfers between devices, local(): lax.all_to_all(help_tiles, 'nbr', split_axis=0, concat_axis=0, tiled=True)  5.64 us
    ppermute x3, starting transfers between devices, local(): from_left.append(lax.ppermute(from_left[-1], 'nbr', plan.right))  4.73 us
  transfers between devices with their start and end apart: 16, of which 3 were waited for; matrix products, arithmetic and copies ran while one was open for 3% of the time, Pallas kernels for 38%

profile of v1, /device:TPU:12, one launch (start us, length us, event | category | flops | bytes accessed | tf_op | source)
XLA Modules:
  0.0 177.4 jit_solution(11242355127004036565)
XLA Ops:
  0.5 1.6 collective-permute-start
  2.0 23.2 %collective-permute-done.3.refs_4_.refs_1_ = f32[16,128,128]{2,1,0:T(8,128)} collective-permute-done((f32[16,128,128]{2,1,0:T(8,128)}, f32[16,128,128]{2,1,0:T(8,128)}, u32[]{:S(2)}, u32[]{:S(2)}) %collective-permute-start.3) | collective-permute-done | bytes 1048608 | tf_op jit(solution)/shard_map/ppermute | solution.py:287
  25.7 1.6 collective-permute-start.1
  27.2 22.3 %collective-permute-done.4.refs_5_.refs_1_ = f32[16,128,128]{2,1,0:T(8,128)} collective-permute-done((f32[16,128,128]{2,1,0:T(8,128)}, f32[16,128,128]{2,1,0:T(8,128)}, u32[]{:S(2)}, u32[]{:S(2)}) %collective-permute-start.4) | collective-permute-done | bytes 1048608 | tf_op jit(solution)/shard_map/ppermute | solution.py:287
  50.0 1.6 collective-permute-start.2
  54.5 6.3 %all-to-all-start = ((s32[8,2,3]{2,1,0:T(2,128)}), s32[8,2,3]{2,1,0:T(2,128)S(1)}, u32[]{:S(2)}, u32[]{:S(2)}) async-start(s32[8,2,3]{2,1,0:T(2,128)} %copy.14), calls=%async_computation | async-start | bytes 16384 | tf_op jit(solution)/shard_map/all_to_all | solution.py:294
  60.8 1.4 collective-permute-start.8
  62.2 14.0 %all-to-all-done = s32[8,2,3]{2,1,0:T(2,128)S(1)} async-done(((s32[8,2,3]{2,1,0:T(2,128)}), s32[8,2,3]{2,1,0:T(2,128)S(1)}, u32[]{:S(2)}, u32[]{:S(2)}) %all-to-all-start) | async-done | bytes 224 | tf_op jit(solution)/shard_map/all_to_all | solution.py:294
  76.2 5.6 %all-to-all-start.1 = ((f32[16,128,128]{2,1,0:T(8,128)}), f32[16,128,128]{2,1,0:T(8,128)}, u32[]{:S(2)}, u32[]{:S(2)}) async-start(f32[16,128,128]{2,1,0:T(8,128)} %param.12), calls=%async_computation.1 | async-start | bytes 2097152 | tf_op jit(solution)/shard_map/all_to_all | solution.py:295
  82.8 2.8 %collective-permute-start.7 = (f32[8,128,128]{2,1,0:T(8,128)}, f32[8,128,128]{2,1,0:T(8,128)}, u32[]{:S(2)}, u32[]{:S(2)}) collective-permute-start(f32[8,128,128]{2,1,0:T(8,128)} %slice.24), channel_id=1, source_target_pairs={{2,0},{7,6},{5,7},{0,1},{10,8},{15,14},{13,15},{8,9},{18,16},{23,2... | collective-permute-start | bytes 1572872 | tf_op jit(solution)/shard_map/ppermute | solution.py:291
  86.5 1.5 collective-permute-start.6
  88.3 4.7 %collective-permute-start.9 = (f32[16,128,128]{2,1,0:T(8,128)}, f32[16,128,128]{2,1,0:T(8,128)}, u32[]{:S(2)}, u32[]{:S(2)}) collective-permute-start(f32[16,128,128]{2,1,0:T(8,128)} %collective-permute-done.3.refs_4_.refs_1_), channel_id=1, source_target_pairs={{5,4},{2,3},{13,12},{10,11},{21,20},{18,19},{29,28},{26,27}} | collective-permute-start | bytes 3145736 | tf_op jit(solution)/shard_map/ppermute | solution.py:289
  93.8 3.3 %stage0.1.refs_3_ = f32[17,128,128]{2,1,0:T(8,128)S(1)} custom-call(s32[6]{0:T(128)S(1)} %convert_reduce_fusion.1.offs, s32[192]{0:T(256)S(1)} %select_reduce_fusion.info, f32[16,128,128]{2,1,0:T(8,128)S(1)} %copy-done.4, f32[192,128,128]{2,1,0:T(8,128)} %refs_15_.1), custom_call_target="tpu_custom_call" | custom-call | flops 100663296 | bytes 8388608 | tf_op jit(solution)/shard_map/stage0/pallas_call | solution.py:370
  97.1 1.0 copy-done.6
  98.3 33.7 %edges.1 = (f32[8,128,128]{2,1,0:T(8,128)}, f32[8,128,128]{2,1,0:T(8,128)}) custom-call(s32[5]{0:T(128)} %stack.39.mode, f32[16,128,128]{2,1,0:T(8,128)} %refs_0_.5, f32[16,128,128]{2,1,0:T(8,128)} %collective-permute-done.refs_1_.refs_0_, f32[16,128,128]{2,1,0:T(8,128)} %collective-permute-done.1.refs_2_.refs_0_, f32[16,128,128]{2,1,0:T(8,128)} %copy-done.2, ...), custom_call_target="tpu_custom_call" | custom-call | tf_op jit(solution)/shard_map/edges/pallas_call | solution.py:383
  132.0 1.9 %collective-permute-start.10 = (f32[8,128,128]{2,1,0:T(8,128)}, f32[8,128,128]{2,1,0:T(8,128)S(1)}, u32[]{:S(2)}, u32[]{:S(2)}) collective-permute-start(f32[8,128,128]{2,1,0:T(8,128)} %get-tuple-element.9), channel_id=1, source_target_pairs={{2,10},{4,12},{6,14},{7,15},{5,13},{3,11},{1,9},{10,18},{12,20},{1... | collective-permute-start | bytes 1572872 | tf_op jit(solution)/shard_map/ppermute | solution.py:393
  134.0 3.6 %collective-permute-start.12 = (f32[8,128,128]{2,1,0:T(8,128)}, f32[8,128,128]{2,1,0:T(8,128)S(1)}, u32[]{:S(2)}, u32[]{:S(2)}) collective-permute-start(f32[8,128,128]{2,1,0:T(8,128)} %get-tuple-element.10), channel_id=1, source_target_pairs={{8,0},{10,2},{12,4},{14,6},{13,5},{11,3},{9,1},{16,8},{18,10},{20,... | collective-permute-start | bytes 1572872 | tf_op jit(solution)/shard_map/ppermute | solution.py:394
  139.2 7.0 %stage1.1.refs_3_ = f32[17,128,128]{2,1,0:T(8,128)S(1)} custom-call(s32[6]{0:T(128)S(1)} %convert_reduce_fusion.1.offs, s32[192]{0:T(256)S(1)} %select_reduce_fusion.info, f32[16,128,128]{2,1,0:T(8,128)} %collective-permute-done.refs_1_.refs_0_, f32[16,128,128]{2,1,0:T(8,128)} %collective-permute-done.3.refs_4_.refs_1_, f32[192,128,128]{2,1,0:T(8,128)} %refs_15_.1, ...), custom_call_target="tpu_custom_call" | custom-call | flops 100663296 | bytes 8388608 | tf_op jit(solution)/shard_map/stage1/pallas_call | solution.py:370
  146.2 7.4 %stage2.1.refs_3_ = f32[17,128,128]{2,1,0:T(8,128)S(1)} custom-call(s32[6]{0:T(128)S(1)} %convert_reduce_fusion.1.offs, s32[192]{0:T(256)S(1)} %select_reduce_fusion.info, f32[16,128,128]{2,1,0:T(8,128)} %collective-permute-done.1.refs_2_.refs_0_, f32[16,128,128]{2,1,0:T(8,128)} %collective-permute-done.4.refs_5_.refs_1_, f32[192,128,128]{2,1,0:T(8,128)} %refs_15_.1, ...), custom_call_target="tpu_custom_call" | custom-call | flops 100663296 | bytes 8388608 | tf_op jit(solution)/shard_map/stage2/pallas_call | solution.py:370
  153.7 5.8 %stage3.1.refs_16_ = f32[17,128,128]{2,1,0:T(8,128)S(1)} custom-call(s32[6]{0:T(128)S(1)} %convert_reduce_fusion.1.offs, s32[192]{0:T(256)S(1)} %select_reduce_fusion.info, f32[16,128,128]{2,1,0:T(8,128)S(1)} %copy-done.3, f32[16,128,128]{2,1,0:T(8,128)S(1)} %copy-done.1, f32[192,128,128]{2,1,0:T(8,128)} %refs_15_.1, f32[17,128,128]{2,1,0:T(8,128)S(1)} %stage2.1.refs_3_), custom_call_target="tpu_custom_call" | custom-call | flops 100663296 | bytes 8388608 | tf_op jit(solution)/shard_map/stage3/pallas_call | solution.py:370
  159.6 1.0 copy-done.8
  160.6 10.9 %last_stage.1 = (f32[17,128,128]{2,1,0:T(8,128)}, f32[16,128,128]{2,1,0:T(8,128)S(1)}) custom-call(s32[6]{0:T(128)S(1)} %convert_reduce_fusion.1.offs, s32[192]{0:T(256)S(1)} %select_reduce_fusion.info, s32[5]{0:T(128)S(1)} %copy-done.10, s32[16]{0:T(128)S(1)} %compare_select_fusion.30.hbuf, s32[16]{0:T(128)S(1)} %get-tuple-element.13.hidx, ...), custom_call_target="tpu_custom_call" | custom-call | flops 100663296 | bytes 8388608 | tf_op jit(solution)/shard_map/last_stage/pallas_call | solution.py:409
  171.6 1.2 copy-done.9
  172.8 4.6 %help.1 = f32[16,128,128]{2,1,0:T(8,128)} custom-call(s32[16]{0:T(128)S(1)} %fusion.12.hrow, f32[16,128,128]{2,1,0:T(8,128)} %all-to-all-done.1.tiles, f32[16,128,128]{2,1,0:T(8,128)S(1)} %get-tuple-element.11.xs, f32[17,128,128]{2,1,0:T(8,128)S(1)} %copy-done.9), custom_call_target="tpu_custom_call" | custom-call | tf_op jit(solution)/shard_map/help/pallas_call | solution.py:420
  (62 shorter events, 9.0 us)
Async XLA Ops:
  0.0 81.8 %copy-start.11 = (s32[192]{0:T(256)S(1)}, s32[192]{0:T(256)}, u32[]{:S(2)}) copy-start(s32[192]{0:T(256)} %param.10) | copy-start | bytes 2308
  0.0 25.2 %collective-permute-start.3 = (f32[16,128,128]{2,1,0:T(8,128)}, f32[16,128,128]{2,1,0:T(8,128)}, u32[]{:S(2)}, u32[]{:S(2)}) collective-permute-start(f32[16,128,128]{2,1,0:T(8,128)} %refs_0_.5), channel_id=1, source_target_pairs={{0,1},{2,0},{4,2},{6,4},{7,6},{5,7},{3,5},{1,3},{8,9},{10,8},{12,1... | collective-permute-start | bytes 3145736 | tf_op jit(solution)/shard_map/ppermute | solution.py:287
  0.5 25.2 %collective-permute-start = (f32[16,128,128]{2,1,0:T(8,128)}, f32[16,128,128]{2,1,0:T(8,128)}, u32[]{:S(2)}, u32[]{:S(2)}) collective-permute-start(f32[16,128,128]{2,1,0:T(8,128)} %refs_0_.5), channel_id=1, source_target_pairs={{0,2},{2,4},{4,6},{6,7},{7,5},{5,3},{3,1},{1,0},{8,10},{10,12},{12... | collective-permute-start | bytes 3145736 | tf_op jit(solution)/shard_map/ppermute | solution.py:286
  25.2 24.3 %collective-permute-start.4 = (f32[16,128,128]{2,1,0:T(8,128)}, f32[16,128,128]{2,1,0:T(8,128)}, u32[]{:S(2)}, u32[]{:S(2)}) collective-permute-start(f32[16,128,128]{2,1,0:T(8,128)} %collective-permute-done.3.refs_4_.refs_1_), channel_id=1, source_target_pairs={{0,1},{2,0},{4,2},{6,4},{7,6},{5,7},{3,5},{1,3},{8,9},{10,8},{12,1... | collective-permute-start | bytes 3145736 | tf_op jit(solution)/shard_map/ppermute | solution.py:287
  25.7 24.3 %collective-permute-start.1 = (f32[16,128,128]{2,1,0:T(8,128)}, f32[16,128,128]{2,1,0:T(8,128)}, u32[]{:S(2)}, u32[]{:S(2)}) collective-permute-start(f32[16,128,128]{2,1,0:T(8,128)} %collective-permute-done.refs_1_.refs_0_), channel_id=1, source_target_pairs={{0,2},{2,4},{4,6},{6,7},{7,5},{5,3},{3,1},{1,0},{8,10},{10,12},{12... | collective-permute-start | bytes 3145736 | tf_op jit(solution)/shard_map/ppermute | solution.py:286
  49.6 32.4 %collective-permute-start.5 = (f32[16,128,128]{2,1,0:T(8,128)}, f32[16,128,128]{2,1,0:T(8,128)S(1)}, u32[]{:S(2)}, u32[]{:S(2)}) collective-permute-start(f32[16,128,128]{2,1,0:T(8,128)} %collective-permute-done.4.refs_5_.refs_1_), channel_id=1, source_target_pairs={{0,1},{2,0},{4,2},{6,4},{7,6},{5,7},{3,5},{1,3},{8,9},{10,8},{12,1... | collective-permute-start | bytes 3145736 | tf_op jit(solution)/shard_map/ppermute | solution.py:287
  50.0 35.6 %collective-permute-start.2 = (f32[16,128,128]{2,1,0:T(8,128)}, f32[16,128,128]{2,1,0:T(8,128)S(1)}, u32[]{:S(2)}, u32[]{:S(2)}) collective-permute-start(f32[16,128,128]{2,1,0:T(8,128)} %collective-permute-done.1.refs_2_.refs_0_), channel_id=1, source_target_pairs={{0,2},{2,4},{4,6},{6,7},{7,5},{5,3},{3,1},{1,0},{8,10},{10,12},{12... | collective-permute-start | bytes 3145736 | tf_op jit(solution)/shard_map/ppermute | solution.py:286
  54.5 21.7 %all-to-all-start = ((s32[8,2,3]{2,1,0:T(2,128)}), s32[8,2,3]{2,1,0:T(2,128)S(1)}, u32[]{:S(2)}, u32[]{:S(2)}) async-start(s32[8,2,3]{2,1,0:T(2,128)} %copy.14), calls=%async_computation | async-start | bytes 16384 | tf_op jit(solution)/shard_map/all_to_all | solution.py:294
  60.8 21.2 %copy-start.12 = (s32[192]{0:T(256)S(1)}, s32[192]{0:T(256)}, u32[]{:S(2)}) copy-start(s32[192]{0:T(256)} %param.11) | copy-start | bytes 2308
  60.8 73.2 %collective-permute-start.8 = (f32[16,128,128]{2,1,0:T(8,128)}, f32[16,128,128]{2,1,0:T(8,128)}, u32[]{:S(2)}, u32[]{:S(2)}) collective-permute-start(f32[16,128,128]{2,1,0:T(8,128)} %collective-permute-done.refs_1_.refs_0_), channel_id=1, source_target_pairs={{3,2},{4,5},{11,10},{12,13},{19,18},{20,21},{27,26},{28,29}} | collective-permute-start | bytes 3145736 | tf_op jit(solution)/shard_map/ppermute | solution.py:288
  76.2 95.3 %all-to-all-start.1 = ((f32[16,128,128]{2,1,0:T(8,128)}), f32[16,128,128]{2,1,0:T(8,128)}, u32[]{:S(2)}, u32[]{:S(2)}) async-start(f32[16,128,128]{2,1,0:T(8,128)} %param.12), calls=%async_computation.1 | async-start | bytes 2097152 | tf_op jit(solution)/shard_map/all_to_all | solution.py:295
  81.9 11.9 %copy-start.4 = (f32[16,128,128]{2,1,0:T(8,128)S(1)}, f32[16,128,128]{2,1,0:T(8,128)}, u32[]{:S(2)}) copy-start(f32[16,128,128]{2,1,0:T(8,128)} %refs_0_.5) | copy-start | bytes 3145732
  82.0 15.1 %copy-start = (f32[16,128,128]{2,1,0:T(8,128)}, f32[16,128,128]{2,1,0:T(8,128)S(1)}, u32[]{:S(2)}) copy-start(f32[16,128,128]{2,1,0:T(8,128)S(1)} %collective-permute-done.5.refs_6_.refs_1_) | copy-start | bytes 3145732
  82.8 54.8 %collective-permute-start.7 = (f32[8,128,128]{2,1,0:T(8,128)}, f32[8,128,128]{2,1,0:T(8,128)}, u32[]{:S(2)}, u32[]{:S(2)}) collective-permute-start(f32[8,128,128]{2,1,0:T(8,128)} %slice.24), channel_id=1, source_target_pairs={{2,0},{7,6},{5,7},{0,1},{10,8},{15,14},{13,15},{8,9},{18,16},{23,2... | collective-permute-start | bytes 1572872 | tf_op jit(solution)/shard_map/ppermute | solution.py:291
  85.7 11.4 %copy-start.2 = (f32[16,128,128]{2,1,0:T(8,128)}, f32[16,128,128]{2,1,0:T(8,128)S(1)}, u32[]{:S(2)}) copy-start(f32[16,128,128]{2,1,0:T(8,128)S(1)} %collective-permute-done.2.refs_3_.refs_0_) | copy-start | bytes 3145732
  86.5 51.8 %collective-permute-start.6 = (f32[8,128,128]{2,1,0:T(8,128)}, f32[8,128,128]{2,1,0:T(8,128)}, u32[]{:S(2)}, u32[]{:S(2)}) collective-permute-start(f32[8,128,128]{2,1,0:T(8,128)} %slice.23), channel_id=1, source_target_pairs={{1,0},{4,6},{6,7},{3,1},{9,8},{12,14},{14,15},{11,9},{17,16},{20,2... | collective-permute-start | bytes 1572872 | tf_op jit(solution)/shard_map/ppermute | solution.py:290
  88.3 72.2 %collective-permute-start.9 = (f32[16,128,128]{2,1,0:T(8,128)}, f32[16,128,128]{2,1,0:T(8,128)}, u32[]{:S(2)}, u32[]{:S(2)}) collective-permute-start(f32[16,128,128]{2,1,0:T(8,128)} %collective-permute-done.3.refs_4_.refs_1_), channel_id=1, source_target_pairs={{5,4},{2,3},{13,12},{10,11},{21,20},{18,19},{29,28},{26,27}} | collective-permute-start | bytes 3145736 | tf_op jit(solution)/shard_map/ppermute | solution.py:289
  98.3 40.9 %copy-start.7 = (f32[17,128,128]{2,1,0:T(8,128)S(1)}, f32[17,128,128]{2,1,0:T(8,128)}, u32[]{:S(2)}) copy-start(f32[17,128,128]{2,1,0:T(8,128)} %copy-done.6) | copy-start | bytes 3342340
  132.0 28.5 %collective-permute-start.10 = (f32[8,128,128]{2,1,0:T(8,128)}, f32[8,128,128]{2,1,0:T(8,128)S(1)}, u32[]{:S(2)}, u32[]{:S(2)}) collective-permute-start(f32[8,128,128]{2,1,0:T(8,128)} %get-tuple-element.9), channel_id=1, source_target_pairs={{2,10},{4,12},{6,14},{7,15},{5,13},{3,11},{1,9},{10,18},{12,20},{1... | collective-permute-start | bytes 1572872 | tf_op jit(solution)/shard_map/ppermute | solution.py:393
  134.0 26.6 %collective-permute-start.12 = (f32[8,128,128]{2,1,0:T(8,128)}, f32[8,128,128]{2,1,0:T(8,128)S(1)}, u32[]{:S(2)}, u32[]{:S(2)}) collective-permute-start(f32[8,128,128]{2,1,0:T(8,128)} %get-tuple-element.10), channel_id=1, source_target_pairs={{8,0},{10,2},{12,4},{14,6},{13,5},{11,3},{9,1},{16,8},{18,10},{20,... | collective-permute-start | bytes 1572872 | tf_op jit(solution)/shard_map/ppermute | solution.py:394
  137.6 22.9 %collective-permute-start.11 = (f32[8,128,128]{2,1,0:T(8,128)}, f32[8,128,128]{2,1,0:T(8,128)S(1)}, u32[]{:S(2)}, u32[]{:S(2)}) collective-permute-start(f32[8,128,128]{2,1,0:T(8,128)} %collective-permute-done.7.refs_8_), channel_id=1, source_target_pairs={{0,8},{8,16},{16,24}} | collective-permute-start | bytes 1572872 | tf_op jit(solution)/shard_map/ppermute | solution.py:405
  138.3 22.2 %collective-permute-start.13 = (f32[8,128,128]{2,1,0:T(8,128)}, f32[8,128,128]{2,1,0:T(8,128)S(1)}, u32[]{:S(2)}, u32[]{:S(2)}) collective-permute-start(f32[8,128,128]{2,1,0:T(8,128)} %collective-permute-done.6.refs_7_), channel_id=1, source_target_pairs={{15,7},{23,15},{31,23}} | collective-permute-start | bytes 1572872 | tf_op jit(solution)/shard_map/ppermute | solution.py:406
  146.2 7.5 %copy-start.1 = (f32[16,128,128]{2,1,0:T(8,128)S(1)}, f32[16,128,128]{2,1,0:T(8,128)}, u32[]{:S(2)}) copy-start(f32[16,128,128]{2,1,0:T(8,128)} %copy-done) | copy-start | bytes 3145732
  146.2 7.5 %copy-start.3 = (f32[16,128,128]{2,1,0:T(8,128)S(1)}, f32[16,128,128]{2,1,0:T(8,128)}, u32[]{:S(2)}) copy-start(f32[16,128,128]{2,1,0:T(8,128)} %copy-done.2) | copy-start | bytes 3145732
  (5 other events, 17.0 us)

commit v2 on v0

v2 whole, which is shorter than its diff:
```python
import functools

import jax
import jax.numpy as jnp
import numpy as np
from jax import lax
from jax.experimental import pallas as pl
from jax.experimental.pallas import tpu as pltpu
from jax.sharding import PartitionSpec as P

RIM = 8
UNROLL = 8
NOTE_ROWS = 8
FAR_PLACE, CUTS, OVER, RIM_FROM, LAST = 4, 6, 10, 12, 14
DEPTH = 4
VMEM_BYTES = 42 << 20
F32 = jnp.float32
I32 = jnp.int32


def grid_of(mesh):
    count = mesh.shape["nbr"]
    try:
        where = np.array([d.coords for d in mesh.devices[0]])
    except AttributeError:
        return [(i, 0) for i in range(count)]
    axes = [a for a in range(where.shape[1]) if len(set(where[:, a])) > 1]
    if len(axes) != 2:
        return [(i, 0) for i in range(count)]
    first, second = axes
    if len(set(where[:, second])) > len(set(where[:, first])):
        first, second = second, first
    where = where - where.min(axis=0)
    return [(int(w[first]), int(w[second])) for w in where]


def ring_of(places):
    index = {place: n for n, place in enumerate(places)}
    rows = max(p[0] for p in places) + 1
    cols = max(p[1] for p in places) + 1
    if len(index) != rows * cols or rows % 2 or cols < 2:
        return list(range(len(places)))
    walk = [(r, 0) for r in range(rows)]
    for step, r in enumerate(reversed(range(rows))):
        across = range(1, cols) if step % 2 == 0 else reversed(range(1, cols))
        walk += [(r, c) for c in across]
    return [index[w] for w in walk]


class Plan:
    def __init__(self, mesh):
        self.groups = mesh.shape["grp"]
        self.count = mesh.shape["nbr"]
        places = grid_of(mesh)
        self.ring = ring_of(places)
        self.pos = [self.ring.index(n) for n in range(self.count)]
        self.half = self.count // 2
        count, half = self.count, self.half
        self.right = self.around([(i, (i + 1) % count) for i in range(count)])
        self.left = self.around([(i, (i - 1) % count) for i in range(count)])
        near = lambda a, b: sum(abs(u - v) for u, v in zip(places[self.ring[a]], places[self.ring[b]])) == 1
        pairs, self.over_r, self.over_l, self.from_right = [], [], [], []
        for i in range(count) if half > 3 else ():
            for members, j in ((self.over_r, (i + 3) % count), (self.over_l, (i - 3) % count)):
                if near(i, j) and all(i != b and j != a for a, b in pairs):
                    pairs.append((j, i))
                    members.append(i)
                    self.from_right += [j] if members is self.over_r else []
        self.over = self.around(pairs)
        self.last_right = self.around([((i - 1) % count, i) for i in range(count) if i not in self.over_r])
        self.last_left = self.around([((i + 1) % count, i) for i in range(count) if i not in self.over_l])

    def around(self, pairs):
        return [(self.ring[a], self.ring[b]) for a, b in pairs]

    def between(self, step, keep):
        return [
            (g * self.count + self.ring[i], (g + step) * self.count + self.ring[i])
            for g in range(self.groups)
            if 0 <= g + step < self.groups
            for i in keep
        ]


def product(a, b):
    a_hi, b_hi = a.astype(jnp.bfloat16), b.astype(jnp.bfloat16)
    a_lo = (a - a_hi.astype(F32)).astype(jnp.bfloat16)
    b_lo = (b - b_hi.astype(F32)).astype(jnp.bfloat16)
    dot = functools.partial(jnp.dot, preferred_element_type=F32)
    return dot(a_hi, b_hi) + (dot(a_lo, b_hi) + dot(a_hi, b_lo))


def run_list(offs, info, stage, bits, fetch_tile, xs, acc, buf, sems, ready):
    slot_bits, row_bits = bits
    total = info.shape[0]
    dump = acc.shape[0] - 1
    first, last = offs[stage], offs[stage + 1]
    groups = lax.div(last - first + (UNROLL - 1), UNROLL)

    def fetch(g):
        s = lax.rem(g, DEPTH)
        for u in range(UNROLL):
            at = jnp.minimum(first + g * UNROLL + u, total - 1)
            fetch_tile(lax.shift_right_logical(info[at], slot_bits + row_bits), buf.at[s, u], sems.at[s]).start()

    for g in range(DEPTH - 1):
        pl.when(g < groups)(functools.partial(fetch, jnp.int32(g)))
    ready()

    def body(g, carry):
        s = lax.rem(g, DEPTH)
        pl.when(g + DEPTH - 1 < groups)(lambda: fetch(g + DEPTH - 1))
        for u in range(UNROLL):
            fetch_tile(0, buf.at[s, u], sems.at[s]).wait()
        rows, terms = [], []
        for u in range(UNROLL):
            at = first + g * UNROLL + u
            entry = info[jnp.minimum(at, total - 1)]
            row = lax.shift_right_logical(entry, slot_bits) & ((1 << row_bits) - 1)
            slot = jnp.where(at < last, entry & ((1 << slot_bits) - 1), 0)
            rows.append(jnp.where(at < last, row, dump))
            terms.append(product(buf[s, u], xs[slot]))
        for row, term in zip(rows, terms):
            acc[row] += term
        return carry

    lax.fori_loop(0, groups, body, 0)


def stage_kernel(stage, bits, layout, helped, *refs):
    refs = list(refs)
    offs, info = refs.pop(0), refs.pop(0)
    hoffs, hinfo = (refs.pop(0), refs.pop(0)) if helped else (None, None)
    mode = refs.pop(0)
    sources = [refs.pop(0) for _ in range(1 + max(c[1] for place in layout for c in place[2]))]
    tiles = refs.pop(0)
    received = refs.pop(0) if helped else None
    before = refs.pop(0) if stage else None
    out, acc, xs, buf, hbuf, xsems, sems, hsems = refs
    rows = acc.shape[0] - 1
    kept = out.shape[0]

    def bring(at, source, start, size, sem):
        return pltpu.make_async_copy(sources[source].at[pl.ds(start, size)], xs.at[pl.ds(at, size)], sem)

    back = None
    if before is not None:
        back = pltpu.make_async_copy(before, acc.at[pl.ds(0, rows)], xsems.at[len(layout)])
        back.start()
    def place_of(at):
        return at if isinstance(at, int) else at[0] + mode[at[1]] * at[2]

    for k, (at, which, choices) in enumerate(layout):
        for value, source, start, size in choices:
            start_it = bring(place_of(at), source, start, size, xsems.at[k]).start
            if which is None:
                start_it()
            else:
                pl.when(mode[which] == value)(start_it)

    def ready():
        if back is None:
            acc[...] = jnp.zeros_like(acc)
        else:
            back.wait()
        for k, (at, _, choices) in enumerate(layout):
            _, source, start, size = choices[0]
            bring(place_of(at), source, start, size, xsems.at[k]).wait()

    def own_tile(t, place, sem):
        return pltpu.make_async_copy(tiles.at[t], place, sem)

    side = tiles.shape[1]

    def help_tile(t, place, sem):
        per = (received.shape[1] - NOTE_ROWS) // side
        chunk = lax.div(t, per)
        start = pl.multiple_of((t - chunk * per) * side, side)
        return pltpu.make_async_copy(received.at[chunk, pl.ds(start, side)], place, sem)

    run_list(offs, info, stage, bits, own_tile, xs, acc, buf, sems, ready)
    if helped:
        run_list(hoffs, hinfo, stage, bits, help_tile, xs, acc, hbuf, hsems, lambda: None)
    out[...] = acc[pl.ds(0, kept)]


def edge_kernel(mode, *refs):
    refs = list(refs)
    low, up, sems = refs[-3:]
    shards = refs[:-4]
    size = shards[0].shape[0]
    for which, out, sem in ((2, low, sems.at[0]), (3, up, sems.at[1])):
        pl.when(mode[which] < 0)(pltpu.make_async_copy(shards[0].at[pl.ds(0, RIM)], out, sem).start)

    def pick(k, ref):
        @pl.when(mode[2] == k)
        def _():
            pltpu.make_async_copy(ref.at[pl.ds(size - RIM, RIM)], low, sems.at[0]).start()

        @pl.when(mode[3] == k)
        def _():
            pltpu.make_async_copy(ref.at[pl.ds(0, RIM)], up, sems.at[1]).start()

    for k, ref in enumerate(shards):
        pick(k, ref)
    pltpu.make_async_copy(shards[0].at[pl.ds(0, RIM)], low, sems.at[0]).wait()
    pltpu.make_async_copy(shards[0].at[pl.ds(0, RIM)], up, sems.at[1]).wait()


def cut_kernel(mode, *refs):
    *shards, first, second, rim, sems = refs
    half = first.shape[0]
    outs = [(first, mode[CUTS], mode[CUTS + 1] * half), (second, mode[CUTS + 2], mode[CUTS + 3] * half)]
    outs.append((rim, jnp.maximum(mode[RIM_FROM], 0), mode[RIM_FROM + 1]))
    for k, (out, which, start) in enumerate(outs):
        for value, ref in enumerate(shards):
            copy = pltpu.make_async_copy(ref.at[pl.ds(start, out.shape[0])], out, sems.at[k])
            pl.when(which == value)(copy.start)
    for k, (out, _, _) in enumerate(outs):
        pltpu.make_async_copy(shards[0].at[pl.ds(0, out.shape[0])], out, sems.at[k]).wait()


def bits_for(n):
    return max(1, (n - 1).bit_length())


SMEM = pl.BlockSpec(memory_space=pltpu.SMEM)
ANY = pl.BlockSpec(memory_space=pl.ANY)
VMEM = pl.BlockSpec(memory_space=pltpu.VMEM)


def table(values, index):
    return sum(jnp.where(index == k, I32(v), I32(0)) for k, v in enumerate(values))


def listed(stage, slot, row, stages, per_stage, bits, kept=None):
    place = stage * per_stage + slot
    rest = (row << bits[0]) | slot
    if kept is not None:
        place, rest = (x[:, :kept].reshape(-1) for x in (place, rest))
    total = place.shape[0]
    number = jnp.arange(total, dtype=I32)
    key = place * total + number
    rank = jnp.sum((key[None, :] < key[:, None]).astype(I32), axis=1)
    entry = (number << (bits[0] + bits[1])) | rest
    info = jnp.sum(jnp.where(rank[:, None] == number[None, :], entry[:, None], 0), axis=0)
    starts = jnp.arange(stages + 1, dtype=I32) * per_stage
    offs = jnp.sum((place[None, :] < starts[:, None]).astype(I32), axis=1)
    return offs, info


def local(plan, sims, own_tiles, own_cols, own_rows, help_tiles, help_cols, help_rows, help_live):
    rows, side, width = sims.shape
    count, half = plan.count, plan.half
    group_rows = rows * count
    cut = rows // 2
    assert rows == 2 * cut and cut >= RIM
    slots = help_tiles.shape[0]
    per_owner = slots // count
    join = min(3, half - 1)
    per_stage = (2 * join + 1) * rows + 2 * RIM
    bits = (bits_for(per_stage), bits_for(rows))
    both = ("grp", "nbr")
    here = table(plan.pos, lax.axis_index("nbr"))

    notes = jnp.stack([help_cols, help_rows, help_live], axis=0).astype(F32).reshape(3, count, per_owner)
    notes = jnp.pad(notes.transpose(1, 0, 2), ((0, 0), (0, NOTE_ROWS - 3), (0, width - per_owner)))
    sent = jnp.concatenate([help_tiles.reshape(count, per_owner * side, width), notes], axis=1)
    received = lax.all_to_all(sent, "nbr", split_axis=0, concat_axis=0, tiled=True)

    place_low, place_up = plan.pos[count - 1], plan.pos[0]

    def away(place):
        return lax.rem(I32(place) - here + count, I32(count))

    low_far = (away(place_low) == half).astype(I32)
    up_far = (away(place_up) == half).astype(I32)

    def locate(cols, least):
        block = cols - RIM
        low, up = block < 0, block >= group_rows
        inside = jnp.clip(block, 0, group_rows - 1)
        shard = inside // rows
        ahead = lax.rem(table(plan.pos, shard) - here + count, I32(count))
        near = jnp.minimum(ahead, count - ahead)
        stage = jnp.maximum(near, least)
        right = ((ahead > 0) & (ahead < half)).astype(I32)
        order = jnp.where(stage == join, jnp.where(near == 0, 0, 2 * near - 1 + right), right)
        slot = inside - shard * rows + order * rows
        slot = jnp.where(low, rows + cols, jnp.where(up, rows + RIM + block - group_rows, slot))
        stage = jnp.where(low, half + low_far, jnp.where(up, half + up_far, stage))
        return stage, slot

    over_r_kind = table([int(i in plan.over_r) for i in range(count)], here)
    over_l_kind = table([int(i in plan.over_l) for i in range(count)], here)

    def edge_source(place):
        ahead = away(place)
        near = jnp.where(ahead == 0, 0, jnp.where(ahead < half, half - 2 + ahead, count - ahead))
        return jnp.where((ahead >= half - 1) & (ahead <= half + 1), -1, near)

    rim_from, rim_row, low_last, up_last = ([-1] * count, [0] * count, [0] * count, [0] * count)
    for place, row, kinds in ((place_low, rows - RIM, low_last), (place_up, 0, up_last)):
        for value, i in ((1, (place - half + 1) % count), (0, (place + half - 1) % count)):
            assert rim_from[i] < 0
            rim_from[i] = 2 if i in (plan.over_l if value else plan.over_r) else value
            rim_row[i], kinds[i] = row, 1

    far_low, far_up = (place_low + half) % count, (place_up + half) % count
    rim_half = [int(i == far_low) for i in range(count)]
    far_half = table(rim_half, here)
    cuts = [
        [2 * int(i in plan.over_r) for i in range(count)],
        [rim_half[(i + 1) % count] for i in range(count)],
        [1 + int(i in plan.over_l) for i in range(count)],
        [1 - rim_half[(i - 1) % count] for i in range(count)],
    ]

    mode = jnp.stack(
        [
            low_far,
            up_far,
            edge_source(place_low),
            edge_source(place_up),
            far_half,
            1 - far_half,
            *(table(values, here) for values in cuts),
            over_r_kind,
            over_l_kind,
            *(table(values, here) for values in (rim_from, rim_row, low_last, up_last)),
        ]
    ).astype(I32)

    offs, info = listed(*locate(own_cols, 0), own_rows, half + 2, per_stage, bits)

    params = pltpu.CompilerParams(vmem_limit_bytes=VMEM_BYTES)
    cost = pl.CostEstimate(
        flops=2 * side * side * width * own_tiles.shape[0] // count, bytes_accessed=8 << 20, transcendentals=0
    )

    def multiply(stage, layout, sources, lists, before):
        helped = len(lists) > 2
        most = max(at + choices[0][3] if isinstance(at, int) else at[0] + 2 * at[2] for at, _, choices in layout)
        given = [*lists, mode, *sources, own_tiles] + ([received] if helped else []) + ([] if before is None else [before])
        tile_slots = lambda: pltpu.VMEM((DEPTH, UNROLL, side, side), F32)
        return pl.pallas_call(
            functools.partial(stage_kernel, stage, bits, layout, helped),
            out_shape=jax.ShapeDtypeStruct((rows, side, width), F32),
            in_specs=[SMEM] * (len(lists) + 1) + [ANY] * (len(given) - len(lists) - 1),
            out_specs=VMEM,
            scratch_shapes=[
                pltpu.VMEM((rows + 1, side, width), F32),
                pltpu.VMEM((most, side, width), F32),
                tile_slots(),
                tile_slots(),
                pltpu.SemaphoreType.DMA((len(layout) + 1,)),
                pltpu.SemaphoreType.DMA((DEPTH,)),
                pltpu.SemaphoreType.DMA((DEPTH,)),
            ],
            compiler_params=params,
            cost_estimate=cost,
            name=f"stage{stage}",
        )(*given)

    whole = lambda k: (k * rows, None, [(0, k, 0, rows)])

    def rims_early(after):
        near_shards = [sims] + from_left[1:] + from_right[1:]
        edge = jax.ShapeDtypeStruct((RIM, side, width), F32)
        low, up = pl.pallas_call(
            edge_kernel,
            out_shape=(edge, edge),
            in_specs=[SMEM] + [ANY] * (len(near_shards) + 1),
            out_specs=(VMEM, VMEM),
            scratch_shapes=[pltpu.SemaphoreType.DMA((2,))],
            compiler_params=params,
            name="edges",
        )(mode, *near_shards, after)
        apart = lambda i, k: min((i - k) % count, (k - i) % count)
        places = lambda place: [k for k in range(count) if apart(k, place) < half - 1]
        low = lax.ppermute(low, both, plan.between(1, places(place_low)))
        up = lax.ppermute(up, both, plan.between(-1, places(place_up)))
        return low, up

    from_left, from_right = [sims], [sims]
    lists, acc, shards = [offs, info], None, [sims]
    for s in range(half):
        if s == join:
            got = received[:, per_owner * side :].astype(I32)
            cols, takes, live = got[:, 0], got[:, 1], got[:, 2]
            stage, slot = locate(cols, join)
            stage = jnp.where(live > 0, stage, half + 2)
            lists = lists + list(listed(stage, slot, takes, half + 2, per_stage, bits, per_owner))
            shards = [sims] + [x for pair in zip(from_left[1:], from_right[1:]) for x in pair]
        if s < half - 1:
            last = s == half - 2
            arriving = [
                lax.ppermute(from_left[-1], "nbr", plan.last_right if last else plan.right),
                lax.ppermute(from_right[-1], "nbr", plan.last_left if last else plan.left),
            ]
            if last:
                gives_right = table([int(i in plan.from_right) for i in range(count)], here) > 0
                over = lax.ppermute(jnp.where(gives_right, from_right[-1], from_left[-1]), "nbr", plan.over)
        else:
            outgoing = pl.pallas_call(
                cut_kernel,
                out_shape=tuple(jax.ShapeDtypeStruct((n, side, width), F32) for n in (cut, cut, RIM)),
                in_specs=[SMEM] + [ANY] * 3,
                out_specs=(VMEM,) * 3,
                scratch_shapes=[pltpu.SemaphoreType.DMA((3,))],
                compiler_params=params,
                name="cut",
            )(mode, from_left[-1], from_right[-1], over)
            arriving = [lax.ppermute(x, "nbr", pairs) for x, pairs in zip(outgoing, (plan.right, plan.left))]
            near_places = lambda place: [(place + half - 1) % count, (place - half + 1) % count]
            pairs = plan.between(1, near_places(place_low)) + plan.between(-1, near_places(place_up))
            rim_last = lax.ppermute(outgoing[2], both, pairs)
        layout = [whole(k) for k in range(len(shards))]
        if s == half - 1:
            amount = len(shards)
            for k in range(2):
                at = amount - 2 + k
                layout[at] = (at * rows, OVER + k, [(0, at, 0, rows), (1, amount, 0, rows)])
            shards = shards + [over]
        acc = multiply(s, layout, shards, lists, acc)
        if s == half - 2:
            low_early, up_early = rims_early(acc)
        ties = [acc, *arriving] + ([received] if s == join - 1 else []) + ([over] if s == half - 2 else [])
        ties = lax.optimization_barrier(ties)
        acc, shards = ties[0], ties[1:3]
        if s == half - 2:
            over = ties[-1]
        if s == join - 1:
            received = ties[3]
        if s < half - 1:
            from_left.append(shards[0])
            from_right.append(shards[1])
    far_a, far_b = shards

    rim_far = lax.ppermute(far_a, both, plan.between(1, [far_low]) + plan.between(-1, [far_up]))

    layout = [
        ((0, FAR_PLACE, cut), None, [(0, 0, 0, cut)]),
        ((0, FAR_PLACE + 1, cut), None, [(0, 1, 0, cut)]),
        (rows, LAST, [(0, 2, 0, RIM), (1, 4, 0, RIM)]),
        (rows + RIM, LAST + 1, [(0, 3, 0, RIM), (1, 4, 0, RIM)]),
    ]
    acc = multiply(half, layout, [far_a, far_b, low_early, up_early, rim_last], lists, acc)
    layout = [(rows, None, [(0, 0, cut - RIM, RIM)]), (rows + RIM, None, [(0, 0, 0, RIM)])]
    return multiply(half + 1, layout, [rim_far], lists, acc)


def solution(mesh):
    spread = P(("grp", "nbr"), None, None)
    flat = P(("grp", "nbr"))
    return jax.shard_map(
        functools.partial(local, Plan(mesh)),
        mesh=mesh,
        in_specs=(spread, spread, flat, flat, spread, flat, flat, flat),
        out_specs=spread,
        check_vma=False,
    )
```

time: 255 us -> 121 us (0.47)
  waiting for transfers between devices: 118 us -> 36.1 us
  matrix products: 48.2 us -> 0 us
  local copies, waits for them, and re-layouts: 51.6 us -> 3.92 us
  Pallas kernels: 0 us -> 33.7 us
  starting transfers between devices: 17.4 us -> 40.7 us
  between operations: 13.5 us -> 0.26 us
    all_gather x1 -> x0, waiting for transfers between devices: 117 us -> none  [local(): group = lax.all_gather(sims, 'nbr', axis=0, tiled=True)]
    dot_general x4 -> x0, matrix products: 48.2 us -> none  [the longest x1 33.8 us: local(): own_terms = jnp.einsum('tij,tjs->tis', own_tiles, own_pick, precision=high)]
    ppermute x2 -> x13, waiting for transfers between devices: 0.01 us -> 36.1 us  [the longest x3 16.1 us: local(): lax.ppermute(from_right[-1], 'nbr', plan.last_left if last else plan.left)]
    pallas_call x0 -> x8, Pallas kernels: none -> 33.7 us  [the longest x6 30 us: multiply(): pl.pallas_call(functools.partial(stage_kernel, stage, bits, layout, helpe...]
    gather x6 -> x0, local copies, waits for them, and re-layouts: 33.1 us -> none  [pick_from(): taken = jnp.take(source, jnp.clip(index, 0, length - 1), axis=0)]
    ppermute x2 -> x13, starting transfers between devices: 5.43 us -> 35.3 us  [the longest x1 14.8 us: rims_early(): low = lax.ppermute(low, both, plan.between(1, places(place_low)))]
    dot_general x1 -> x0, local copies, waits for them, and re-layouts: 12.8 us -> none  [local(): own_terms = jnp.einsum('tij,tjs->tis', own_tiles, own_pick, precision=high)]
    all_to_all x2 -> x1, starting transfers between devices: 12 us -> 5.44 us  [local(): lax.all_to_all(sent, 'nbr', split_axis=0, concat_axis=0, tiled=True)]
  transfers between devices with their start and end apart: 5 -> 14, of which waited for: 1 -> 7; matrix products, arithmetic and copies ran while one was open for 37% -> 5% of each run, Pallas kernels for 0% -> 24%
where the time goes in v2:
time: 121 us; the launch traced here: 120 us
  starting transfers between devices  40.7 us (34%)
  waiting for transfers between devices  36.1 us (30%)
  Pallas kernels  33.7 us (28%)
  other arithmetic  5.34 us (4%)
  local copies, waits for them, and re-layouts  3.92 us (3%)
    pallas_call x6, Pallas kernels, multiply(): pl.pallas_call(functools.partial(stage_kernel, stage, bits, layout, helpe...  30 us
    ppermute x3, waiting for transfers between devices, local(): lax.ppermute(from_right[-1], 'nbr', plan.last_left if last else plan.left)  16.1 us
    ppermute x3, waiting for transfers between devices, local(): lax.ppermute(from_left[-1], 'nbr', plan.last_right if last else plan.right)  15 us
    ppermute x1, starting transfers between devices, rims_early(): low = lax.ppermute(low, both, plan.between(1, places(place_low)))  14.8 us
    ppermute x1, starting transfers between devices, local(): lax.ppermute(far_a, both, plan.between(1, [far_low]) + plan.between(-1, [...  5.89 us
    all_to_all x1, starting transfers between devices, local(): lax.all_to_all(sent, 'nbr', split_axis=0, concat_axis=0, tiled=True)  5.44 us
    ppermute x3, starting transfers between devices, local(): lax.ppermute(from_left[-1], 'nbr', plan.last_right if last else plan.right)  5.23 us
    unnamed x22, local copies, waits for them, and re-layouts  3.44 us
  transfers between devices with their start and end apart: 14, of which 7 were waited for; matrix products, arithmetic and copies ran while one was open for 5% of the time, Pallas kernels for 24%

profile of v2, /device:TPU:27, one launch (start us, length us, event | category | flops | bytes accessed | tf_op | source)
XLA Modules:
  0.0 120.0 jit_solution(7826914243584052797)
XLA Ops:
  0.3 1.2 %collective-permute-start = (f32[16,128,128]{2,1,0:T(8,128)}, f32[16,128,128]{2,1,0:T(8,128)}, u32[]{:S(2)}, u32[]{:S(2)}) collective-permute-start(f32[16,128,128]{2,1,0:T(8,128)} %refs_0_.1), channel_id=1, source_target_pairs={{0,2},{2,4},{4,6},{6,7},{7,5},{5,3},{3,1},{1,0},{8,10},{10,12},{12... | collective-permute-start | bytes 3145736 | tf_op jit(solution)/shard_map/ppermute | solution.py:398
  4.2 1.2 %copy-done.2 = f32[16,128,128]{2,1,0:T(8,128)S(1)} copy-done((f32[16,128,128]{2,1,0:T(8,128)S(1)}, f32[16,128,128]{2,1,0:T(8,128)}, u32[]{:S(2)}) %copy-start.2) | copy-done | bytes 1048600
  5.4 2.7 %stage0.1.refs_6_ = f32[16,128,128]{2,1,0:T(8,128)S(1)} custom-call(s32[7]{0:T(128)S(1)} %convert_reduce_fusion.2.refs_0_, s32[192]{0:T(256)S(1)} %select_reduce_fusion.refs_1_, s32[16]{0:T(128)S(1)} %stack.79.refs_2_.refs_4_.mode, f32[16,128,128]{2,1,0:T(8,128)S(1)} %copy-done.2, f32[192,128,128]{2,1,0:T(8,128)} %refs_6_.1), custom_call_target="tpu_custom_call" | custom-call | flops 100663296 | bytes 8388608 | tf_op jit(solution)/shard_map/stage0/pallas_call | solution.py:346
  9.1 15.3 %collective-permute-done.1.refs_4_.refs_7_.refs_3_ = f32[16,128,128]{2,1,0:T(8,128)} collective-permute-done((f32[16,128,128]{2,1,0:T(8,128)}, f32[16,128,128]{2,1,0:T(8,128)}, u32[]{:S(2)}, u32[]{:S(2)}) %collective-permute-start.1) | collective-permute-done | bytes 1048608 | tf_op jit(solution)/shard_map/ppermute | solution.py:399
  27.2 5.4 %all-to-all-start = ((f32[8,264,128]{2,1,0:T(8,128)}), f32[8,264,128]{2,1,0:T(8,128)S(1)}, u32[]{:S(2)}, u32[]{:S(2)}) async-start(f32[8,264,128]{2,1,0:T(8,128)} %select_maximum_fusion), calls=%async_computation | async-start | bytes 2162688 | tf_op jit(solution)/shard_map/all_to_all | solution.py:269
  32.6 1.2 %copy-done.6 = f32[16,128,128]{2,1,0:T(8,128)S(1)} copy-done((f32[16,128,128]{2,1,0:T(8,128)S(1)}, f32[16,128,128]{2,1,0:T(8,128)}, u32[]{:S(2)}) %copy-start.6) | copy-done | bytes 1048600
  33.8 5.8 %stage1.1.refs_6_ = f32[16,128,128]{2,1,0:T(8,128)S(1)} custom-call(s32[7]{0:T(128)S(1)} %convert_reduce_fusion.2.refs_0_, s32[192]{0:T(256)S(1)} %select_reduce_fusion.refs_1_, s32[16]{0:T(128)S(1)} %stack.79.refs_2_.refs_4_.mode, f32[16,128,128]{2,1,0:T(8,128)} %collective-permute-done.refs_3_.refs_6_.refs_1_, ...), custom_call_target="tpu_custom_call" | custom-call | flops 100663296 | bytes 8388608 | tf_op jit(solution)/shard_map/stage1/pallas_call | solution.py:346
  39.6 7.8 %collective-permute-done.2.refs_3_.refs_8_.refs_2_ = f32[16,128,128]{2,1,0:T(8,128)S(1)} collective-permute-done((f32[16,128,128]{2,1,0:T(8,128)}, f32[16,128,128]{2,1,0:T(8,128)S(1)}, u32[]{:S(2)}, u32[]{:S(2)}) %collective-permute-start.2) | collective-permute-done | bytes 1048608 | tf_op jit(solution)/shard_map/ppermute | solution.py:398
  49.3 1.8 %collective-permute-start.6 = (f32[16,128,128]{2,1,0:T(8,128)}, f32[16,128,128]{2,1,0:T(8,128)}, u32[]{:S(2)}, u32[]{:S(2)}) collective-permute-start(f32[16,128,128]{2,1,0:T(8,128)} %broadcast_select_fusion), channel_id=1, source_target_pairs={{3,2},{5,4},{4,5},{2,3},{11,10},{13,12},{12,13},{10,11},{19,18},{2... | collective-permute-start | bytes 3145736 | tf_op jit(solution)/shard_map/ppermute | solution.py:403
  51.1 2.9 %collective-permute-start.4 = (f32[16,128,128]{2,1,0:T(8,128)S(1)}, f32[16,128,128]{2,1,0:T(8,128)}, u32[]{:S(2)}, u32[]{:S(2)}) collective-permute-start(f32[16,128,128]{2,1,0:T(8,128)S(1)} %collective-permute-done.2.refs_3_.refs_8_.refs_2_), channel_id=1, source_target_pairs={{1,0},{0,2},{4,6},{6,7},{7,5},{3,1},{9,8},{8,10},{12,14},{14,15},{... | collective-permute-start | bytes 3145736 | tf_op jit(solution)/shard_map/ppermute | solution.py:398
  54.0 2.4 %collective-permute-start.5 = (f32[16,128,128]{2,1,0:T(8,128)S(1)}, f32[16,128,128]{2,1,0:T(8,128)}, u32[]{:S(2)}, u32[]{:S(2)}) collective-permute-start(f32[16,128,128]{2,1,0:T(8,128)S(1)} %collective-permute-done.3.refs_4_.refs_9_), channel_id=1, source_target_pairs={{2,0},{6,4},{7,6},{5,7},{1,3},{0,1},{10,8},{14,12},{15,14},{13,15}... | collective-permute-start | bytes 3145736 | tf_op jit(solution)/shard_map/ppermute | solution.py:399
  56.4 4.5 %stage2.1.refs_15_.refs_5_ = f32[16,128,128]{2,1,0:T(8,128)S(1)} custom-call(s32[7]{0:T(128)S(1)} %convert_reduce_fusion.2.refs_0_, s32[192]{0:T(256)S(1)} %select_reduce_fusion.refs_1_, s32[16]{0:T(128)S(1)} %stack.79.refs_2_.refs_4_.mode, f32[16,128,128]{2,1,0:T(8,128)S(1)} %collective-permute-done.2.refs_3_.refs_8_.refs_2_, ...), custom_call_target="tpu_custom_call" | custom-call | flops 100663296 | bytes 8388608 | tf_op jit(solution)/shard_map/stage2/pallas_call | solution.py:346
  60.9 1.7 %edges.1 = (f32[8,128,128]{2,1,0:T(8,128)}, f32[8,128,128]{2,1,0:T(8,128)}) custom-call(s32[16]{0:T(128)S(1)} %stack.79.refs_2_.refs_4_.mode, f32[16,128,128]{2,1,0:T(8,128)S(1)} %copy-done.3, f32[16,128,128]{2,1,0:T(8,128)} %collective-permute-done.refs_3_.refs_6_.refs_1_, f32[16,128,128]{2,1,0:T(8,128)S(1)} %collective-permute-done.2.refs_3_.refs_8_.refs_2_, ...), custom_call_target="tpu_custom_call" | custom-call | tf_op jit(solution)/shard_map/edges/pallas_call | solution.py:370
  62.7 14.8 %collective-permute-start.10 = (f32[8,128,128]{2,1,0:T(8,128)}, f32[8,128,128]{2,1,0:T(8,128)}, u32[]{:S(2)}, u32[]{:S(2)}) collective-permute-start(f32[8,128,128]{2,1,0:T(8,128)} %get-tuple-element.39), channel_id=1, source_target_pairs={{4,12},{6,14},{7,15},{5,13},{3,11},{12,20},{14,22},{15,23},{13,21}... | collective-permute-start | bytes 1572872 | tf_op jit(solution)/shard_map/ppermute | solution.py:381
  77.5 1.5 %collective-permute-start.11 = (f32[8,128,128]{2,1,0:T(8,128)}, f32[8,128,128]{2,1,0:T(8,128)}, u32[]{:S(2)}, u32[]{:S(2)}) collective-permute-start(f32[8,128,128]{2,1,0:T(8,128)} %get-tuple-element.40), channel_id=1, source_target_pairs={{8,0},{10,2},{12,4},{11,3},{9,1},{16,8},{18,10},{20,12},{19,11},{1... | collective-permute-start | bytes 1572872 | tf_op jit(solution)/shard_map/ppermute | solution.py:382
  79.0 7.2 %collective-permute-done.4.refs_10_.refs_0_ = f32[16,128,128]{2,1,0:T(8,128)} collective-permute-done((f32[16,128,128]{2,1,0:T(8,128)S(1)}, f32[16,128,128]{2,1,0:T(8,128)}, u32[]{:S(2)}, u32[]{:S(2)}) %collective-permute-start.4) | collective-permute-done | bytes 1048608 | tf_op jit(solution)/shard_map/ppermute | solution.py:398
  86.5 2.0 %cut.1 = (f32[8,128,128]{2,1,0:T(8,128)S(1)}, f32[8,128,128]{2,1,0:T(8,128)S(1)}, f32[8,128,128]{2,1,0:T(8,128)S(1)}) custom-call(s32[16]{0:T(128)S(1)} %stack.79.refs_2_.refs_4_.mode, f32[16,128,128]{2,1,0:T(8,128)} %collective-permute-done.4.refs_10_.refs_0_, f32[16,128,128]{2,1,0:T(8,128)} %collective-permute-done.5.refs_11_.refs_1_, ...), custom_call_target="tpu_custom_call" | custom-call | tf_op jit(solution)/shard_map/cut/pallas_call | solution.py:405
  88.5 2.4 %collective-permute-start.7 = (f32[8,128,128]{2,1,0:T(8,128)S(1)}, f32[8,128,128]{2,1,0:T(8,128)S(1)}, u32[]{:S(2)}, u32[]{:S(2)}) collective-permute-start(f32[8,128,128]{2,1,0:T(8,128)S(1)} %get-tuple-element.35), channel_id=1, source_target_pairs={{0,2},{2,4},{4,6},{6,7},{7,5},{5,3},{3,1},{1,0},{8,10},{10,12},{12... | collective-permute-start | bytes 1572872 | tf_op jit(solution)/shard_map/ppermute | solution.py:414
  92.1 6.8 %stage3.1.refs_12_ = f32[16,128,128]{2,1,0:T(8,128)S(1)} custom-call(s32[7]{0:T(128)S(1)} %convert_reduce_fusion.2.refs_0_, s32[192]{0:T(256)S(1)} %select_reduce_fusion.refs_1_, s32[7]{0:T(128)S(1)} %convert_reduce_fusion.3.refs_2_, s32[16]{0:T(128)S(1)} %select_reduce_fusion.1.refs_3_, s32[16]{0:T(128)S(1)} %stack.79.refs_2_.refs_4_.mode, ...), custom_call_target="tpu_custom_call" | custom-call | flops 100663296 | bytes 8388608 | tf_op jit(solution)/shard_map/stage3/pallas_call | solution.py:346
  99.3 1.9 %collective-permute-done.8.refs_6_ = f32[8,128,128]{2,1,0:T(8,128)S(1)} collective-permute-done((f32[8,128,128]{2,1,0:T(8,128)S(1)}, f32[8,128,128]{2,1,0:T(8,128)S(1)}, u32[]{:S(2)}, u32[]{:S(2)}) %collective-permute-start.8) | collective-permute-done | bytes 524320 | tf_op jit(solution)/shard_map/ppermute | solution.py:414
  101.2 5.9 %collective-permute-start.9 = (f32[8,128,128]{2,1,0:T(8,128)S(1)}, f32[8,128,128]{2,1,0:T(8,128)S(1)}, u32[]{:S(2)}, u32[]{:S(2)}) collective-permute-start(f32[8,128,128]{2,1,0:T(8,128)S(1)} %collective-permute-done.7.refs_5_), channel_id=1, source_target_pairs={{0,8},{8,16},{16,24},{15,7},{23,15},{31,23}} | collective-permute-start | bytes 1572872 | tf_op jit(solution)/shard_map/ppermute | solution.py:440
  107.2 5.4 %stage4.1.refs_8_ = f32[16,128,128]{2,1,0:T(8,128)S(1)} custom-call(s32[7]{0:T(128)S(1)} %convert_reduce_fusion.2.refs_0_, s32[192]{0:T(256)S(1)} %select_reduce_fusion.refs_1_, s32[7]{0:T(128)S(1)} %convert_reduce_fusion.3.refs_2_, s32[16]{0:T(128)S(1)} %select_reduce_fusion.1.refs_3_, s32[16]{0:T(128)S(1)} %stack.79.refs_2_.refs_4_.mode, ...), custom_call_target="tpu_custom_call" | custom-call | flops 100663296 | bytes 8388608 | tf_op jit(solution)/shard_map/stage4/pallas_call | solution.py:346
  112.6 2.5 %collective-permute-done.9.refs_5_ = f32[8,128,128]{2,1,0:T(8,128)S(1)} collective-permute-done((f32[8,128,128]{2,1,0:T(8,128)S(1)}, f32[8,128,128]{2,1,0:T(8,128)S(1)}, u32[]{:S(2)}, u32[]{:S(2)}) %collective-permute-start.9) | collective-permute-done | bytes 524320 | tf_op jit(solution)/shard_map/ppermute | solution.py:440
  115.1 4.9 %stage5.1 = f32[16,128,128]{2,1,0:T(8,128)} custom-call(s32[7]{0:T(128)S(1)} %convert_reduce_fusion.2.refs_0_, s32[192]{0:T(256)S(1)} %select_reduce_fusion.refs_1_, s32[7]{0:T(128)S(1)} %convert_reduce_fusion.3.refs_2_, s32[16]{0:T(128)S(1)} %select_reduce_fusion.1.refs_3_, s32[16]{0:T(128)S(1)} %stack.79.refs_2_.refs_4_.mode, ...), custom_call_target="tpu_custom_call" | custom-call | flops 100663296 | bytes 8388608 | tf_op jit(solution)/shard_map/stage5/pallas_call | solution.py:346
  (59 shorter events, 10.5 us)
Async XLA Ops:
  0.0 24.3 %collective-permute-start.1 = (f32[16,128,128]{2,1,0:T(8,128)}, f32[16,128,128]{2,1,0:T(8,128)}, u32[]{:S(2)}, u32[]{:S(2)}) collective-permute-start(f32[16,128,128]{2,1,0:T(8,128)} %refs_0_.1), channel_id=1, source_target_pairs={{0,1},{2,0},{4,2},{6,4},{7,6},{5,7},{3,5},{1,3},{8,9},{10,8},{12,1... | collective-permute-start | bytes 3145736 | tf_op jit(solution)/shard_map/ppermute | solution.py:399
  0.3 24.1 %collective-permute-start = (f32[16,128,128]{2,1,0:T(8,128)}, f32[16,128,128]{2,1,0:T(8,128)}, u32[]{:S(2)}, u32[]{:S(2)}) collective-permute-start(f32[16,128,128]{2,1,0:T(8,128)} %refs_0_.1), channel_id=1, source_target_pairs={{0,2},{2,4},{4,6},{6,7},{7,5},{5,3},{3,1},{1,0},{8,10},{10,12},{12... | collective-permute-start | bytes 3145736 | tf_op jit(solution)/shard_map/ppermute | solution.py:398
  4.2 1.2 %copy-start.2 = (f32[16,128,128]{2,1,0:T(8,128)S(1)}, f32[16,128,128]{2,1,0:T(8,128)}, u32[]{:S(2)}) copy-start(f32[16,128,128]{2,1,0:T(8,128)} %refs_0_.1) | copy-start | bytes 3145732
  5.4 20.4 %copy-start.8 = (s32[16]{0:T(128)S(1)}, s32[16]{0:T(128)}, u32[]{:S(2)}) copy-start(s32[16]{0:T(128)} %param.13) | copy-start | bytes 196
  5.4 20.5 %copy-start.9 = (s32[16]{0:T(128)S(1)}, s32[16]{0:T(128)}, u32[]{:S(2)}) copy-start(s32[16]{0:T(128)} %param.14) | copy-start | bytes 196
  5.4 20.6 %copy-start.10 = (s32[16]{0:T(128)S(1)}, s32[16]{0:T(128)}, u32[]{:S(2)}) copy-start(s32[16]{0:T(128)} %param.15) | copy-start | bytes 196
  5.4 20.7 %copy-start.7 = (f32[16,128,128]{2,1,0:T(8,128)S(1)}, f32[16,128,128]{2,1,0:T(8,128)}, u32[]{:S(2)}) copy-start(f32[16,128,128]{2,1,0:T(8,128)} %param.12) | copy-start | bytes 3145732
  24.3 23.1 %collective-permute-start.2 = (f32[16,128,128]{2,1,0:T(8,128)}, f32[16,128,128]{2,1,0:T(8,128)S(1)}, u32[]{:S(2)}, u32[]{:S(2)}) collective-permute-start(f32[16,128,128]{2,1,0:T(8,128)} %collective-permute-done.refs_3_.refs_6_.refs_1_), channel_id=1, source_target_pairs={{0,2},{2,4},{4,6},{6,7},{7,5},{5,3},{3,1},{1,0},{8,10},{10,12},{12... | collective-permute-start | bytes 3145736 | tf_op jit(solution)/shard_map/ppermute | solution.py:398
  25.5 22.7 %collective-permute-start.3 = (f32[16,128,128]{2,1,0:T(8,128)}, f32[16,128,128]{2,1,0:T(8,128)S(1)}, u32[]{:S(2)}, u32[]{:S(2)}) collective-permute-start(f32[16,128,128]{2,1,0:T(8,128)} %collective-permute-done.1.refs_4_.refs_7_.refs_3_), channel_id=1, source_target_pairs={{0,1},{2,0},{4,2},{6,4},{7,6},{5,7},{3,5},{1,3},{8,9},{10,8},{12,1... | collective-permute-start | bytes 3145736 | tf_op jit(solution)/shard_map/ppermute | solution.py:399
  27.2 51.8 %all-to-all-start = ((f32[8,264,128]{2,1,0:T(8,128)}), f32[8,264,128]{2,1,0:T(8,128)S(1)}, u32[]{:S(2)}, u32[]{:S(2)}) async-start(f32[8,264,128]{2,1,0:T(8,128)} %select_maximum_fusion), calls=%async_computation | async-start | bytes 2162688 | tf_op jit(solution)/shard_map/all_to_all | solution.py:269
  32.6 1.2 %copy-start.6 = (f32[16,128,128]{2,1,0:T(8,128)S(1)}, f32[16,128,128]{2,1,0:T(8,128)}, u32[]{:S(2)}) copy-start(f32[16,128,128]{2,1,0:T(8,128)} %copy-done.5) | copy-start | bytes 3145732
  49.3 11.6 %copy-start.3 = (f32[16,128,128]{2,1,0:T(8,128)S(1)}, f32[16,128,128]{2,1,0:T(8,128)}, u32[]{:S(2)}) copy-start(f32[16,128,128]{2,1,0:T(8,128)} %refs_0_.1) | copy-start | bytes 3145732
  49.3 29.7 %collective-permute-start.6 = (f32[16,128,128]{2,1,0:T(8,128)}, f32[16,128,128]{2,1,0:T(8,128)}, u32[]{:S(2)}, u32[]{:S(2)}) collective-permute-start(f32[16,128,128]{2,1,0:T(8,128)} %broadcast_select_fusion), channel_id=1, source_target_pairs={{3,2},{5,4},{4,5},{2,3},{11,10},{13,12},{12,13},{10,11},{19,18},{2... | collective-permute-start | bytes 3145736 | tf_op jit(solution)/shard_map/ppermute | solution.py:403
  51.1 35.1 %collective-permute-start.4 = (f32[16,128,128]{2,1,0:T(8,128)S(1)}, f32[16,128,128]{2,1,0:T(8,128)}, u32[]{:S(2)}, u32[]{:S(2)}) collective-permute-start(f32[16,128,128]{2,1,0:T(8,128)S(1)} %collective-permute-done.2.refs_3_.refs_8_.refs_2_), channel_id=1, source_target_pairs={{1,0},{0,2},{4,6},{6,7},{7,5},{3,1},{9,8},{8,10},{12,14},{14,15},{... | collective-permute-start | bytes 3145736 | tf_op jit(solution)/shard_map/ppermute | solution.py:398
  54.0 32.2 %collective-permute-start.5 = (f32[16,128,128]{2,1,0:T(8,128)S(1)}, f32[16,128,128]{2,1,0:T(8,128)}, u32[]{:S(2)}, u32[]{:S(2)}) collective-permute-start(f32[16,128,128]{2,1,0:T(8,128)S(1)} %collective-permute-done.3.refs_4_.refs_9_), channel_id=1, source_target_pairs={{2,0},{6,4},{7,6},{5,7},{1,3},{0,1},{10,8},{14,12},{15,14},{13,15}... | collective-permute-start | bytes 3145736 | tf_op jit(solution)/shard_map/ppermute | solution.py:399
  60.9 1.8 %copy-start = (f32[16,128,128]{2,1,0:T(8,128)}, f32[16,128,128]{2,1,0:T(8,128)S(1)}, u32[]{:S(2)}) copy-start(f32[16,128,128]{2,1,0:T(8,128)S(1)} %stage2.1.refs_15_.refs_5_) | copy-start | bytes 3145732
  62.7 44.5 %collective-permute-start.10 = (f32[8,128,128]{2,1,0:T(8,128)}, f32[8,128,128]{2,1,0:T(8,128)}, u32[]{:S(2)}, u32[]{:S(2)}) collective-permute-start(f32[8,128,128]{2,1,0:T(8,128)} %get-tuple-element.39), channel_id=1, source_target_pairs={{4,12},{6,14},{7,15},{5,13},{3,11},{12,20},{14,22},{15,23},{13,21}... | collective-permute-start | bytes 1572872 | tf_op jit(solution)/shard_map/ppermute | solution.py:381
  77.5 29.6 %collective-permute-start.11 = (f32[8,128,128]{2,1,0:T(8,128)}, f32[8,128,128]{2,1,0:T(8,128)}, u32[]{:S(2)}, u32[]{:S(2)}) collective-permute-start(f32[8,128,128]{2,1,0:T(8,128)} %get-tuple-element.40), channel_id=1, source_target_pairs={{8,0},{10,2},{12,4},{11,3},{9,1},{16,8},{18,10},{20,12},{19,11},{1... | collective-permute-start | bytes 1572872 | tf_op jit(solution)/shard_map/ppermute | solution.py:382
  86.5 5.5 %copy-start.1 = (f32[16,128,128]{2,1,0:T(8,128)S(1)}, f32[16,128,128]{2,1,0:T(8,128)}, u32[]{:S(2)}) copy-start(f32[16,128,128]{2,1,0:T(8,128)} %copy-done) | copy-start | bytes 3145732
  86.5 5.5 %copy-start.4 = (f32[16,128,128]{2,1,0:T(8,128)S(1)}, f32[16,128,128]{2,1,0:T(8,128)}, u32[]{:S(2)}) copy-start(f32[16,128,128]{2,1,0:T(8,128)} %refs_0_.1) | copy-start | bytes 3145732
  88.5 10.8 %collective-permute-start.7 = (f32[8,128,128]{2,1,0:T(8,128)S(1)}, f32[8,128,128]{2,1,0:T(8,128)S(1)}, u32[]{:S(2)}, u32[]{:S(2)}) collective-permute-start(f32[8,128,128]{2,1,0:T(8,128)S(1)} %get-tuple-element.35), channel_id=1, source_target_pairs={{0,2},{2,4},{4,6},{6,7},{7,5},{5,3},{3,1},{1,0},{8,10},{10,12},{12... | collective-permute-start | bytes 1572872 | tf_op jit(solution)/shard_map/ppermute | solution.py:414
  90.9 10.4 %collective-permute-start.8 = (f32[8,128,128]{2,1,0:T(8,128)S(1)}, f32[8,128,128]{2,1,0:T(8,128)S(1)}, u32[]{:S(2)}, u32[]{:S(2)}) collective-permute-start(f32[8,128,128]{2,1,0:T(8,128)S(1)} %get-tuple-element.36), channel_id=1, source_target_pairs={{0,1},{2,0},{4,2},{6,4},{7,6},{5,7},{3,5},{1,3},{8,9},{10,8},{12,1... | collective-permute-start | bytes 1572872 | tf_op jit(solution)/shard_map/ppermute | solution.py:414
  90.9 16.3 %collective-permute-start.12 = (f32[8,128,128]{2,1,0:T(8,128)S(1)}, f32[8,128,128]{2,1,0:T(8,128)S(1)}, u32[]{:S(2)}, u32[]{:S(2)}) collective-permute-start(f32[8,128,128]{2,1,0:T(8,128)S(1)} %get-tuple-element.41), channel_id=1, source_target_pairs={{1,9},{2,10},{9,17},{10,18},{17,25},{18,26},{14,6},{13,5},{22,14},... | collective-permute-start | bytes 1572872 | tf_op jit(solution)/shard_map/ppermute | solution.py:417
  101.2 13.9 %collective-permute-start.9 = (f32[8,128,128]{2,1,0:T(8,128)S(1)}, f32[8,128,128]{2,1,0:T(8,128)S(1)}, u32[]{:S(2)}, u32[]{:S(2)}) collective-permute-start(f32[8,128,128]{2,1,0:T(8,128)S(1)} %collective-permute-done.7.refs_5_), channel_id=1, source_target_pairs={{0,8},{8,16},{16,24},{15,7},{23,15},{31,23}} | collective-permute-start | bytes 1572872 | tf_op jit(solution)/shard_map/ppermute | solution.py:440
  (1 other events, 1.0 us)

commit v3 on v2

--- a/solution.py
+++ b/solution.py
@@ -425,6 +425,10 @@
         acc = multiply(s, layout, shards, lists, acc)
         if s == half - 2:
             low_early, up_early = rims_early(acc)
+        if s == half - 1:
+            acc, far_a = lax.optimization_barrier((acc, arriving[0]))
+            far_b = arriving[1]
+            break
         ties = [acc, *arriving] + ([received] if s == join - 1 else []) + ([over] if s == half - 2 else [])
         ties = lax.optimization_barrier(ties)
         acc, shards = ties[0], ties[1:3]
@@ -435,7 +439,6 @@
         if s < half - 1:
             from_left.append(shards[0])
             from_right.append(shards[1])
-    far_a, far_b = shards
 
     rim_far = lax.ppermute(far_a, both, plan.between(1, [far_low]) + plan.between(-1, [far_up]))
 

time: 121 us -> 120 us (level)
  waiting for transfers between devices: 36.1 us -> 33.6 us
  starting transfers between devices: 40.7 us -> 42 us
    ppermute x2, waiting for transfers between devices: 2.39 us -> 0.01 us  [local(): lax.ppermute(x, 'nbr', pairs)]
    ppermute x1, starting transfers between devices: 14.8 us -> 16.1 us  [rims_early(): low = lax.ppermute(low, both, plan.between(1, places(place_low)))]
  transfers between devices with their start and end apart: 14 -> 14, of which waited for: 7 -> 5; matrix products, arithmetic and copies ran while one was open for 5% -> 5% of each run, Pallas kernels for 24% -> 25%
where the time goes in v3:
time: 120 us
  starting transfers between devices  42 us (35%)
  Pallas kernels  34.8 us (29%)
  waiting for transfers between devices  33.6 us (28%)
  other arithmetic  5.34 us (4%)
  local copies, waits for them, and re-layouts  3.92 us (3%)
    pallas_call x6, Pallas kernels, multiply(): pl.pallas_call(functools.partial(stage_kernel, stage, bits, layout, helpe...  31.1 us
    ppermute x1, starting transfers between devices, rims_early(): low = lax.ppermute(low, both, plan.between(1, places(place_low)))  16.1 us
    ppermute x3, waiting for transfers between devices, local(): lax.ppermute(from_right[-1], 'nbr', plan.last_left if last else plan.left)  15.7 us
    ppermute x3, waiting for transfers between devices, local(): lax.ppermute(from_left[-1], 'nbr', plan.last_right if last else plan.right)  14.6 us
    ppermute x1, starting transfers between devices, local(): lax.ppermute(far_a, both, plan.between(1, [far_low]) + plan.between(-1, [...  5.91 us
    all_to_all x1, starting transfers between devices, local(): lax.all_to_all(sent, 'nbr', split_axis=0, concat_axis=0, tiled=True)  5.44 us
    ppermute x3, starting transfers between devices, local(): lax.ppermute(from_left[-1], 'nbr', plan.last_right if last else plan.right)  5.23 us
    unnamed x22, local copies, waits for them, and re-layouts  3.44 us
  transfers between devices with their start and end apart: 14, of which 5 were waited for; matrix products, arithmetic and copies ran while one was open for 5% of the time, Pallas kernels for 25%

profile of v3, /device:TPU:27, one launch (start us, length us, event | category | flops | bytes accessed | tf_op | source)
XLA Modules:
  0.0 119.9 jit_solution(16663460611763164005)
XLA Ops:
  0.3 1.2 %collective-permute-start = (f32[16,128,128]{2,1,0:T(8,128)}, f32[16,128,128]{2,1,0:T(8,128)}, u32[]{:S(2)}, u32[]{:S(2)}) collective-permute-start(f32[16,128,128]{2,1,0:T(8,128)} %refs_0_.1), channel_id=1, source_target_pairs={{0,2},{2,4},{4,6},{6,7},{7,5},{5,3},{3,1},{1,0},{8,10},{10,12},{12... | collective-permute-start | bytes 3145736 | tf_op jit(solution)/shard_map/ppermute | solution.py:398
  4.2 1.2 %copy-done.2 = f32[16,128,128]{2,1,0:T(8,128)S(1)} copy-done((f32[16,128,128]{2,1,0:T(8,128)S(1)}, f32[16,128,128]{2,1,0:T(8,128)}, u32[]{:S(2)}) %copy-start.2) | copy-done | bytes 1048600
  5.4 3.1 %stage0.1.refs_6_ = f32[16,128,128]{2,1,0:T(8,128)S(1)} custom-call(s32[7]{0:T(128)S(1)} %convert_reduce_fusion.2.refs_0_, s32[192]{0:T(256)S(1)} %select_reduce_fusion.refs_1_, s32[16]{0:T(128)S(1)} %stack.79.refs_2_.refs_4_.mode, f32[16,128,128]{2,1,0:T(8,128)S(1)} %copy-done.2, f32[192,128,128]{2,1,0:T(8,128)} %refs_6_.1), custom_call_target="tpu_custom_call" | custom-call | flops 100663296 | bytes 8388608 | tf_op jit(solution)/shard_map/stage0/pallas_call | solution.py:346
  9.5 14.9 %collective-permute-done.1.refs_4_.refs_7_.refs_3_ = f32[16,128,128]{2,1,0:T(8,128)} collective-permute-done((f32[16,128,128]{2,1,0:T(8,128)}, f32[16,128,128]{2,1,0:T(8,128)}, u32[]{:S(2)}, u32[]{:S(2)}) %collective-permute-start.1) | collective-permute-done | bytes 1048608 | tf_op jit(solution)/shard_map/ppermute | solution.py:399
  24.3 1.1 collective-permute-start.2
  27.2 5.4 %all-to-all-start = ((f32[8,264,128]{2,1,0:T(8,128)}), f32[8,264,128]{2,1,0:T(8,128)S(1)}, u32[]{:S(2)}, u32[]{:S(2)}) async-start(f32[8,264,128]{2,1,0:T(8,128)} %select_maximum_fusion), calls=%async_computation | async-start | bytes 2162688 | tf_op jit(solution)/shard_map/all_to_all | solution.py:269
  32.6 1.2 %copy-done.6 = f32[16,128,128]{2,1,0:T(8,128)S(1)} copy-done((f32[16,128,128]{2,1,0:T(8,128)S(1)}, f32[16,128,128]{2,1,0:T(8,128)}, u32[]{:S(2)}) %copy-start.6) | copy-done | bytes 1048600
  33.8 5.4 %stage1.1.refs_6_ = f32[16,128,128]{2,1,0:T(8,128)S(1)} custom-call(s32[7]{0:T(128)S(1)} %convert_reduce_fusion.2.refs_0_, s32[192]{0:T(256)S(1)} %select_reduce_fusion.refs_1_, s32[16]{0:T(128)S(1)} %stack.79.refs_2_.refs_4_.mode, f32[16,128,128]{2,1,0:T(8,128)} %collective-permute-done.refs_3_.refs_6_.refs_1_, ...), custom_call_target="tpu_custom_call" | custom-call | flops 100663296 | bytes 8388608 | tf_op jit(solution)/shard_map/stage1/pallas_call | solution.py:346
  39.2 8.2 %collective-permute-done.2.refs_3_.refs_8_.refs_2_ = f32[16,128,128]{2,1,0:T(8,128)S(1)} collective-permute-done((f32[16,128,128]{2,1,0:T(8,128)}, f32[16,128,128]{2,1,0:T(8,128)S(1)}, u32[]{:S(2)}, u32[]{:S(2)}) %collective-permute-start.2) | collective-permute-done | bytes 1048608 | tf_op jit(solution)/shard_map/ppermute | solution.py:398
  49.3 1.8 %collective-permute-start.6 = (f32[16,128,128]{2,1,0:T(8,128)}, f32[16,128,128]{2,1,0:T(8,128)}, u32[]{:S(2)}, u32[]{:S(2)}) collective-permute-start(f32[16,128,128]{2,1,0:T(8,128)} %broadcast_select_fusion), channel_id=1, source_target_pairs={{3,2},{5,4},{4,5},{2,3},{11,10},{13,12},{12,13},{10,11},{19,18},{2... | collective-permute-start | bytes 3145736 | tf_op jit(solution)/shard_map/ppermute | solution.py:403
  51.1 2.9 %collective-permute-start.4 = (f32[16,128,128]{2,1,0:T(8,128)S(1)}, f32[16,128,128]{2,1,0:T(8,128)}, u32[]{:S(2)}, u32[]{:S(2)}) collective-permute-start(f32[16,128,128]{2,1,0:T(8,128)S(1)} %collective-permute-done.2.refs_3_.refs_8_.refs_2_), channel_id=1, source_target_pairs={{1,0},{0,2},{4,6},{6,7},{7,5},{3,1},{9,8},{8,10},{12,14},{14,15},{... | collective-permute-start | bytes 3145736 | tf_op jit(solution)/shard_map/ppermute | solution.py:398
  54.0 2.4 %collective-permute-start.5 = (f32[16,128,128]{2,1,0:T(8,128)S(1)}, f32[16,128,128]{2,1,0:T(8,128)}, u32[]{:S(2)}, u32[]{:S(2)}) collective-permute-start(f32[16,128,128]{2,1,0:T(8,128)S(1)} %collective-permute-done.3.refs_4_.refs_9_), channel_id=1, source_target_pairs={{2,0},{6,4},{7,6},{5,7},{1,3},{0,1},{10,8},{14,12},{15,14},{13,15}... | collective-permute-start | bytes 3145736 | tf_op jit(solution)/shard_map/ppermute | solution.py:399
  56.4 4.0 %stage2.1.refs_15_.refs_5_ = f32[16,128,128]{2,1,0:T(8,128)S(1)} custom-call(s32[7]{0:T(128)S(1)} %convert_reduce_fusion.2.refs_0_, s32[192]{0:T(256)S(1)} %select_reduce_fusion.refs_1_, s32[16]{0:T(128)S(1)} %stack.79.refs_2_.refs_4_.mode, f32[16,128,128]{2,1,0:T(8,128)S(1)} %collective-permute-done.2.refs_3_.refs_8_.refs_2_, ...), custom_call_target="tpu_custom_call" | custom-call | flops 100663296 | bytes 8388608 | tf_op jit(solution)/shard_map/stage2/pallas_call | solution.py:346
  60.5 1.7 %edges.1 = (f32[8,128,128]{2,1,0:T(8,128)}, f32[8,128,128]{2,1,0:T(8,128)}) custom-call(s32[16]{0:T(128)S(1)} %stack.79.refs_2_.refs_4_.mode, f32[16,128,128]{2,1,0:T(8,128)S(1)} %copy-done.3, f32[16,128,128]{2,1,0:T(8,128)} %collective-permute-done.refs_3_.refs_6_.refs_1_, f32[16,128,128]{2,1,0:T(8,128)S(1)} %collective-permute-done.2.refs_3_.refs_8_.refs_2_, ...), custom_call_target="tpu_custom_call" | custom-call | tf_op jit(solution)/shard_map/edges/pallas_call | solution.py:370
  62.2 16.1 %collective-permute-start.10 = (f32[8,128,128]{2,1,0:T(8,128)}, f32[8,128,128]{2,1,0:T(8,128)}, u32[]{:S(2)}, u32[]{:S(2)}) collective-permute-start(f32[8,128,128]{2,1,0:T(8,128)} %get-tuple-element.37), channel_id=1, source_target_pairs={{4,12},{6,14},{7,15},{5,13},{3,11},{12,20},{14,22},{15,23},{13,21}... | collective-permute-start | bytes 1572872 | tf_op jit(solution)/shard_map/ppermute | solution.py:381
  78.3 1.5 %collective-permute-start.11 = (f32[8,128,128]{2,1,0:T(8,128)}, f32[8,128,128]{2,1,0:T(8,128)}, u32[]{:S(2)}, u32[]{:S(2)}) collective-permute-start(f32[8,128,128]{2,1,0:T(8,128)} %get-tuple-element.38), channel_id=1, source_target_pairs={{8,0},{10,2},{12,4},{11,3},{9,1},{16,8},{18,10},{20,12},{19,11},{1... | collective-permute-start | bytes 1572872 | tf_op jit(solution)/shard_map/ppermute | solution.py:382
  79.8 6.4 %collective-permute-done.4.refs_10_.refs_0_ = f32[16,128,128]{2,1,0:T(8,128)} collective-permute-done((f32[16,128,128]{2,1,0:T(8,128)S(1)}, f32[16,128,128]{2,1,0:T(8,128)}, u32[]{:S(2)}, u32[]{:S(2)}) %collective-permute-start.4) | collective-permute-done | bytes 1048608 | tf_op jit(solution)/shard_map/ppermute | solution.py:398
  86.5 2.0 %cut.1 = (f32[8,128,128]{2,1,0:T(8,128)S(1)}, f32[8,128,128]{2,1,0:T(8,128)S(1)}, f32[8,128,128]{2,1,0:T(8,128)S(1)}) custom-call(s32[16]{0:T(128)S(1)} %stack.79.refs_2_.refs_4_.mode, f32[16,128,128]{2,1,0:T(8,128)} %collective-permute-done.4.refs_10_.refs_0_, f32[16,128,128]{2,1,0:T(8,128)} %collective-permute-done.5.refs_11_.refs_1_, ...), custom_call_target="tpu_custom_call" | custom-call | tf_op jit(solution)/shard_map/cut/pallas_call | solution.py:405
  88.5 2.4 %collective-permute-start.7 = (f32[8,128,128]{2,1,0:T(8,128)S(1)}, f32[8,128,128]{2,1,0:T(8,128)S(1)}, u32[]{:S(2)}, u32[]{:S(2)}) collective-permute-start(f32[8,128,128]{2,1,0:T(8,128)S(1)} %get-tuple-element.34), channel_id=1, source_target_pairs={{0,2},{2,4},{4,6},{6,7},{7,5},{5,3},{3,1},{1,0},{8,10},{10,12},{12... | collective-permute-start | bytes 1572872 | tf_op jit(solution)/shard_map/ppermute | solution.py:414
  92.1 7.9 %stage3.1.refs_12_ = f32[16,128,128]{2,1,0:T(8,128)S(1)} custom-call(s32[7]{0:T(128)S(1)} %convert_reduce_fusion.2.refs_0_, s32[192]{0:T(256)S(1)} %select_reduce_fusion.refs_1_, s32[7]{0:T(128)S(1)} %convert_reduce_fusion.3.refs_2_, s32[16]{0:T(128)S(1)} %select_reduce_fusion.1.refs_3_, s32[16]{0:T(128)S(1)} %stack.79.refs_2_.refs_4_.mode, ...), custom_call_target="tpu_custom_call" | custom-call | flops 100663296 | bytes 8388608 | tf_op jit(solution)/shard_map/stage3/pallas_call | solution.py:346
  100.0 5.9 %collective-permute-start.8 = (f32[8,128,128]{2,1,0:T(8,128)S(1)}, f32[8,128,128]{2,1,0:T(8,128)S(1)}, u32[]{:S(2)}, u32[]{:S(2)}) collective-permute-start(f32[8,128,128]{2,1,0:T(8,128)S(1)} %collective-permute-done.7.refs_5_), channel_id=1, source_target_pairs={{0,8},{8,16},{16,24},{15,7},{23,15},{31,23}} | collective-permute-start | bytes 1572872 | tf_op jit(solution)/shard_map/ppermute | solution.py:443
  106.0 5.4 %stage4.1.refs_8_ = f32[16,128,128]{2,1,0:T(8,128)S(1)} custom-call(s32[7]{0:T(128)S(1)} %convert_reduce_fusion.2.refs_0_, s32[192]{0:T(256)S(1)} %select_reduce_fusion.refs_1_, s32[7]{0:T(128)S(1)} %convert_reduce_fusion.3.refs_2_, s32[16]{0:T(128)S(1)} %select_reduce_fusion.1.refs_3_, s32[16]{0:T(128)S(1)} %stack.79.refs_2_.refs_4_.mode, ...), custom_call_target="tpu_custom_call" | custom-call | flops 100663296 | bytes 8388608 | tf_op jit(solution)/shard_map/stage4/pallas_call | solution.py:346
  111.4 3.3 %collective-permute-done.8.refs_5_ = f32[8,128,128]{2,1,0:T(8,128)S(1)} collective-permute-done((f32[8,128,128]{2,1,0:T(8,128)S(1)}, f32[8,128,128]{2,1,0:T(8,128)S(1)}, u32[]{:S(2)}, u32[]{:S(2)}) %collective-permute-start.8) | collective-permute-done | bytes 524320 | tf_op jit(solution)/shard_map/ppermute | solution.py:443
  114.6 5.3 %stage5.1 = f32[16,128,128]{2,1,0:T(8,128)} custom-call(s32[7]{0:T(128)S(1)} %convert_reduce_fusion.2.refs_0_, s32[192]{0:T(256)S(1)} %select_reduce_fusion.refs_1_, s32[7]{0:T(128)S(1)} %convert_reduce_fusion.3.refs_2_, s32[16]{0:T(128)S(1)} %select_reduce_fusion.1.refs_3_, s32[16]{0:T(128)S(1)} %stack.79.refs_2_.refs_4_.mode, ...), custom_call_target="tpu_custom_call" | custom-call | flops 100663296 | bytes 8388608 | tf_op jit(solution)/shard_map/stage5/pallas_call | solution.py:346
  (59 shorter events, 8.9 us)
Async XLA Ops:
  0.0 24.3 %collective-permute-start.1 = (f32[16,128,128]{2,1,0:T(8,128)}, f32[16,128,128]{2,1,0:T(8,128)}, u32[]{:S(2)}, u32[]{:S(2)}) collective-permute-start(f32[16,128,128]{2,1,0:T(8,128)} %refs_0_.1), channel_id=1, source_target_pairs={{0,1},{2,0},{4,2},{6,4},{7,6},{5,7},{3,5},{1,3},{8,9},{10,8},{12,1... | collective-permute-start | bytes 3145736 | tf_op jit(solution)/shard_map/ppermute | solution.py:399
  0.3 24.1 %collective-permute-start = (f32[16,128,128]{2,1,0:T(8,128)}, f32[16,128,128]{2,1,0:T(8,128)}, u32[]{:S(2)}, u32[]{:S(2)}) collective-permute-start(f32[16,128,128]{2,1,0:T(8,128)} %refs_0_.1), channel_id=1, source_target_pairs={{0,2},{2,4},{4,6},{6,7},{7,5},{5,3},{3,1},{1,0},{8,10},{10,12},{12... | collective-permute-start | bytes 3145736 | tf_op jit(solution)/shard_map/ppermute | solution.py:398
  4.2 1.2 %copy-start.2 = (f32[16,128,128]{2,1,0:T(8,128)S(1)}, f32[16,128,128]{2,1,0:T(8,128)}, u32[]{:S(2)}) copy-start(f32[16,128,128]{2,1,0:T(8,128)} %refs_0_.1) | copy-start | bytes 3145732
  5.4 20.4 %copy-start.8 = (s32[16]{0:T(128)S(1)}, s32[16]{0:T(128)}, u32[]{:S(2)}) copy-start(s32[16]{0:T(128)} %param.13) | copy-start | bytes 196
  5.4 20.5 %copy-start.9 = (s32[16]{0:T(128)S(1)}, s32[16]{0:T(128)}, u32[]{:S(2)}) copy-start(s32[16]{0:T(128)} %param.14) | copy-start | bytes 196
  5.4 20.6 %copy-start.10 = (s32[16]{0:T(128)S(1)}, s32[16]{0:T(128)}, u32[]{:S(2)}) copy-start(s32[16]{0:T(128)} %param.15) | copy-start | bytes 196
  5.4 20.7 %copy-start.7 = (f32[16,128,128]{2,1,0:T(8,128)S(1)}, f32[16,128,128]{2,1,0:T(8,128)}, u32[]{:S(2)}) copy-start(f32[16,128,128]{2,1,0:T(8,128)} %param.12) | copy-start | bytes 3145732
  24.3 23.1 %collective-permute-start.2 = (f32[16,128,128]{2,1,0:T(8,128)}, f32[16,128,128]{2,1,0:T(8,128)S(1)}, u32[]{:S(2)}, u32[]{:S(2)}) collective-permute-start(f32[16,128,128]{2,1,0:T(8,128)} %collective-permute-done.refs_3_.refs_6_.refs_1_), channel_id=1, source_target_pairs={{0,2},{2,4},{4,6},{6,7},{7,5},{5,3},{3,1},{1,0},{8,10},{10,12},{12... | collective-permute-start | bytes 3145736 | tf_op jit(solution)/shard_map/ppermute | solution.py:398
  25.5 22.7 %collective-permute-start.3 = (f32[16,128,128]{2,1,0:T(8,128)}, f32[16,128,128]{2,1,0:T(8,128)S(1)}, u32[]{:S(2)}, u32[]{:S(2)}) collective-permute-start(f32[16,128,128]{2,1,0:T(8,128)} %collective-permute-done.1.refs_4_.refs_7_.refs_3_), channel_id=1, source_target_pairs={{0,1},{2,0},{4,2},{6,4},{7,6},{5,7},{3,5},{1,3},{8,9},{10,8},{12,1... | collective-permute-start | bytes 3145736 | tf_op jit(solution)/shard_map/ppermute | solution.py:399
  27.2 52.7 %all-to-all-start = ((f32[8,264,128]{2,1,0:T(8,128)}), f32[8,264,128]{2,1,0:T(8,128)S(1)}, u32[]{:S(2)}, u32[]{:S(2)}) async-start(f32[8,264,128]{2,1,0:T(8,128)} %select_maximum_fusion), calls=%async_computation | async-start | bytes 2162688 | tf_op jit(solution)/shard_map/all_to_all | solution.py:269
  32.6 1.2 %copy-start.6 = (f32[16,128,128]{2,1,0:T(8,128)S(1)}, f32[16,128,128]{2,1,0:T(8,128)}, u32[]{:S(2)}) copy-start(f32[16,128,128]{2,1,0:T(8,128)} %copy-done.5) | copy-start | bytes 3145732
  49.3 11.1 %copy-start.3 = (f32[16,128,128]{2,1,0:T(8,128)S(1)}, f32[16,128,128]{2,1,0:T(8,128)}, u32[]{:S(2)}) copy-start(f32[16,128,128]{2,1,0:T(8,128)} %refs_0_.1) | copy-start | bytes 3145732
  49.3 30.5 %collective-permute-start.6 = (f32[16,128,128]{2,1,0:T(8,128)}, f32[16,128,128]{2,1,0:T(8,128)}, u32[]{:S(2)}, u32[]{:S(2)}) collective-permute-start(f32[16,128,128]{2,1,0:T(8,128)} %broadcast_select_fusion), channel_id=1, source_target_pairs={{3,2},{5,4},{4,5},{2,3},{11,10},{13,12},{12,13},{10,11},{19,18},{2... | collective-permute-start | bytes 3145736 | tf_op jit(solution)/shard_map/ppermute | solution.py:403
  51.1 35.1 %collective-permute-start.4 = (f32[16,128,128]{2,1,0:T(8,128)S(1)}, f32[16,128,128]{2,1,0:T(8,128)}, u32[]{:S(2)}, u32[]{:S(2)}) collective-permute-start(f32[16,128,128]{2,1,0:T(8,128)S(1)} %collective-permute-done.2.refs_3_.refs_8_.refs_2_), channel_id=1, source_target_pairs={{1,0},{0,2},{4,6},{6,7},{7,5},{3,1},{9,8},{8,10},{12,14},{14,15},{... | collective-permute-start | bytes 3145736 | tf_op jit(solution)/shard_map/ppermute | solution.py:398
  54.0 32.2 %collective-permute-start.5 = (f32[16,128,128]{2,1,0:T(8,128)S(1)}, f32[16,128,128]{2,1,0:T(8,128)}, u32[]{:S(2)}, u32[]{:S(2)}) collective-permute-start(f32[16,128,128]{2,1,0:T(8,128)S(1)} %collective-permute-done.3.refs_4_.refs_9_), channel_id=1, source_target_pairs={{2,0},{6,4},{7,6},{5,7},{1,3},{0,1},{10,8},{14,12},{15,14},{13,15}... | collective-permute-start | bytes 3145736 | tf_op jit(solution)/shard_map/ppermute | solution.py:399
  60.5 1.8 %copy-start = (f32[16,128,128]{2,1,0:T(8,128)}, f32[16,128,128]{2,1,0:T(8,128)S(1)}, u32[]{:S(2)}) copy-start(f32[16,128,128]{2,1,0:T(8,128)S(1)} %stage2.1.refs_15_.refs_5_) | copy-start | bytes 3145732
  62.2 43.7 %collective-permute-start.10 = (f32[8,128,128]{2,1,0:T(8,128)}, f32[8,128,128]{2,1,0:T(8,128)}, u32[]{:S(2)}, u32[]{:S(2)}) collective-permute-start(f32[8,128,128]{2,1,0:T(8,128)} %get-tuple-element.37), channel_id=1, source_target_pairs={{4,12},{6,14},{7,15},{5,13},{3,11},{12,20},{14,22},{15,23},{13,21}... | collective-permute-start | bytes 1572872 | tf_op jit(solution)/shard_map/ppermute | solution.py:381
  78.3 27.6 %collective-permute-start.11 = (f32[8,128,128]{2,1,0:T(8,128)}, f32[8,128,128]{2,1,0:T(8,128)}, u32[]{:S(2)}, u32[]{:S(2)}) collective-permute-start(f32[8,128,128]{2,1,0:T(8,128)} %get-tuple-element.38), channel_id=1, source_target_pairs={{8,0},{10,2},{12,4},{11,3},{9,1},{16,8},{18,10},{20,12},{19,11},{1... | collective-permute-start | bytes 1572872 | tf_op jit(solution)/shard_map/ppermute | solution.py:382
  86.5 5.5 %copy-start.1 = (f32[16,128,128]{2,1,0:T(8,128)S(1)}, f32[16,128,128]{2,1,0:T(8,128)}, u32[]{:S(2)}) copy-start(f32[16,128,128]{2,1,0:T(8,128)} %copy-done) | copy-start | bytes 3145732
  86.5 5.5 %copy-start.4 = (f32[16,128,128]{2,1,0:T(8,128)S(1)}, f32[16,128,128]{2,1,0:T(8,128)}, u32[]{:S(2)}) copy-start(f32[16,128,128]{2,1,0:T(8,128)} %refs_0_.1) | copy-start | bytes 3145732
  88.5 11.4 %collective-permute-start.7 = (f32[8,128,128]{2,1,0:T(8,128)S(1)}, f32[8,128,128]{2,1,0:T(8,128)S(1)}, u32[]{:S(2)}, u32[]{:S(2)}) collective-permute-start(f32[8,128,128]{2,1,0:T(8,128)S(1)} %get-tuple-element.34), channel_id=1, source_target_pairs={{0,2},{2,4},{4,6},{6,7},{7,5},{5,3},{3,1},{1,0},{8,10},{10,12},{12... | collective-permute-start | bytes 1572872 | tf_op jit(solution)/shard_map/ppermute | solution.py:414
  90.9 15.0 %collective-permute-start.9 = (f32[8,128,128]{2,1,0:T(8,128)S(1)}, f32[8,128,128]{2,1,0:T(8,128)S(1)}, u32[]{:S(2)}, u32[]{:S(2)}) collective-permute-start(f32[8,128,128]{2,1,0:T(8,128)S(1)} %get-tuple-element.36), channel_id=1, source_target_pairs={{0,1},{2,0},{4,2},{6,4},{7,6},{5,7},{3,5},{1,3},{8,9},{10,8},{12,1... | collective-permute-start | bytes 1572872 | tf_op jit(solution)/shard_map/ppermute | solution.py:414
  90.9 15.0 %collective-permute-start.12 = (f32[8,128,128]{2,1,0:T(8,128)S(1)}, f32[8,128,128]{2,1,0:T(8,128)S(1)}, u32[]{:S(2)}, u32[]{:S(2)}) collective-permute-start(f32[8,128,128]{2,1,0:T(8,128)S(1)} %get-tuple-element.39), channel_id=1, source_target_pairs={{1,9},{2,10},{9,17},{10,18},{17,25},{18,26},{14,6},{13,5},{22,14},... | collective-permute-start | bytes 1572872 | tf_op jit(solution)/shard_map/ppermute | solution.py:417
  100.0 14.6 %collective-permute-start.8 = (f32[8,128,128]{2,1,0:T(8,128)S(1)}, f32[8,128,128]{2,1,0:T(8,128)S(1)}, u32[]{:S(2)}, u32[]{:S(2)}) collective-permute-start(f32[8,128,128]{2,1,0:T(8,128)S(1)} %collective-permute-done.7.refs_5_), channel_id=1, source_target_pairs={{0,8},{8,16},{16,24},{15,7},{23,15},{31,23}} | collective-permute-start | bytes 1572872 | tf_op jit(solution)/shard_map/ppermute | solution.py:443
  (1 other events, 1.0 us)
